TPU v7x, 256 devices: a whole 4x4x8 slice. The times are simulated.
256 devices in a mesh: obs: 16 (over z, x_hi), cells: 16 (over y, x_lo, core).
Axes of the slice: x: 4 (x_hi: 2, x_lo: 2; x = x_hi * 2 + x_lo), y: 4, z: 8, core: 2. Of those that a mesh axis runs over, the one named last changes fastest.
Arguments:
- adjoint_start: float32 [4096, 16, 8, 128], P('obs', 'cells'), may hold values from -8 to 8
- forward_heads: float32 [64, 16, 8, 128], P(None, 'cells'), may hold values from -6 to 6
- zone_label: int32 [16, 8, 128], P('cells'), may hold values from 0 to 15
- zone_logk: float32 [16], replicated, may hold values from -1.2 to 1.2
- obs_cell: int32 [4096], P('obs'), may hold values from 0 to 16383
- test_of_obs: int32 [4096], P('obs'), may hold values from 0 to 63
Outputs:
- sensitivity: float32 [4096, 16, 8, 128], P('obs', 'cells')
- gram: float32 [4096, 4096], P('obs', 'cells')
All inputs are finite; a program needn't handle non-finite values.
Results may differ from a plain program's by a relative error of at most 0.0003.
Values sent between devices are 32-bit elements; how exact they have to be, the bound alone decides.
No kernel may reach another device: no remote copies, remote signals or barrier semaphores. Data moves between devices by JAX's collectives and lax.ppermute only.
A program may use at most 64 MiB of HBM per device.

v0:
```python
import jax
import jax.numpy as jnp
from jax import lax
from jax.sharding import PartitionSpec as P

SWEEPS = 3


source_weight = 16.0
spectrum_centre = 1.075
spectrum_halfwidth = 0.925


def with_halo(block, sides, width):
    for axis, dim in sides:
        count = lax.axis_size(axis)
        forward = [(i, i + 1) for i in range(count - 1)]
        backward = [(target, source) for source, target in forward]
        low = lax.ppermute(
            lax.slice_in_dim(block, block.shape[dim] - width, None, axis=dim), axis, forward
        )
        high = lax.ppermute(lax.slice_in_dim(block, 0, width, axis=dim), axis, backward)
        block = jnp.concatenate([low, block, high], axis=dim)
    return block


def conductivity(zone_label, zone_logk):
    table = jnp.exp(zone_logk)
    labels = jnp.arange(table.shape[0], dtype=jnp.int32)
    match = zone_label[None] == labels[:, None, None, None]
    return jnp.sum(jnp.where(match, table[:, None, None, None], jnp.float32(0.0)), axis=0)


def face(centre, beside):
    return jnp.where(beside > 0, 2.0 * centre * beside / (centre + beside), centre)


def neighbours(padded):
    return [
        padded[..., :-2, 1:-1, 1:-1],
        padded[..., 2:, 1:-1, 1:-1],
        padded[..., 1:-1, :-2, 1:-1],
        padded[..., 1:-1, 2:, 1:-1],
        padded[..., 1:-1, 1:-1, :-2],
        padded[..., 1:-1, 1:-1, 2:],
    ]


def face_weights(cond_padded):
    centre = cond_padded[1:-1, 1:-1, 1:-1]
    weights = [face(centre, beside) for beside in neighbours(cond_padded)]
    diagonal = weights[0]
    for extra in weights[1:]:
        diagonal = diagonal + extra
    return (weights, diagonal)


def operate(padded, field, weights, diagonal):
    result = diagonal * field
    for weight, beside in zip(weights, neighbours(padded)):
        result = result - weight * beside
    return result


def gradients(padded):
    return [
        (padded[..., 2:, 1:-1, 1:-1] - padded[..., :-2, 1:-1, 1:-1]) * 0.5,
        (padded[..., 1:-1, 2:, 1:-1] - padded[..., 1:-1, :-2, 1:-1]) * 0.5,
        (padded[..., 1:-1, 1:-1, 2:] - padded[..., 1:-1, 1:-1, :-2]) * 0.5,
    ]


def pad_sides(rimmed):
    return jnp.pad(rimmed, ((0, 0), (0, 0), (1, 1), (1, 1)))


def sweep_padding(field):
    return pad_sides(with_halo(field, (("cells", 1),), 1))


def chebyshev(start, sources, weights, diagonal):
    ratio = spectrum_centre / spectrum_halfwidth
    adjoint = start
    update = None
    damping = 1.0 / ratio
    for sweep in range(SWEEPS):
        misfit = sources - operate(sweep_padding(adjoint), adjoint, weights, diagonal)
        if sweep == 0:
            update = misfit / (spectrum_centre * diagonal)
            damping = 1.0 / ratio
        else:
            newer = 1.0 / (2.0 * ratio - damping)
            update = newer * damping * update + 2.0 * newer / spectrum_halfwidth * (
                misfit / diagonal
            )
            damping = newer
        adjoint = adjoint + update
    return adjoint


def product_rows(left, right):
    return lax.dot_general(
        left,
        right,
        (((1,), (1,)), ((), ())),
        preferred_element_type=jnp.float32,
        precision=lax.Precision.HIGHEST,
    )


def per_device(adjoint_start, forward_heads, zone_label, zone_logk, obs_cell, test_of_obs):
    layers, rows_y, rows_z = zone_label.shape
    width = layers * rows_y * rows_z
    conduct = conductivity(zone_label, zone_logk)
    stacked = jnp.concatenate([conduct[None], forward_heads], axis=0)
    rimmed = with_halo(stacked, (("cells", 1),), 1)
    padded = pad_sides(rimmed)
    weights, diagonal = face_weights(padded[0])
    head_grads = gradients(padded[1:])
    offset = lax.axis_index("cells") * width
    cell_ids = (offset + jnp.arange(width, dtype=jnp.int32)).reshape(layers, rows_y, rows_z)
    sources = jnp.where(
        cell_ids[None] == obs_cell[:, None, None, None],
        jnp.float32(source_weight),
        jnp.float32(0.0),
    )
    adjoint = chebyshev(adjoint_start, sources, weights, diagonal)
    adjoint_padded = pad_sides(with_halo(adjoint, (("cells", 1),), 1))
    adjoint_grads = gradients(adjoint_padded)
    total = adjoint_grads[0] * jnp.take(head_grads[0], test_of_obs, axis=0)
    total = total + adjoint_grads[1] * jnp.take(head_grads[1], test_of_obs, axis=0)
    total = total + adjoint_grads[2] * jnp.take(head_grads[2], test_of_obs, axis=0)
    sensitivity = -conduct * total
    group = sensitivity.shape[0]
    panel = sensitivity.reshape(group, width)
    partial_value = product_rows(panel, lax.all_gather(panel, "obs", axis=0, tiled=True))
    slabs = lax.axis_size("cells")
    summed = lax.psum(partial_value, "cells")
    share = summed.shape[1] // slabs
    mine = lax.dynamic_slice_in_dim(summed, lax.axis_index("cells") * share, share, 1)
    gram = mine * (1.0 / (width * slabs))
    return (sensitivity, gram)


def solution(mesh):
    return jax.shard_map(
        per_device,
        mesh=mesh,
        in_specs=(
            P("obs", "cells", None, None),
            P(None, "cells", None, None),
            P("cells", None, None),
            P(),
            P("obs"),
            P("obs"),
        ),
        out_specs=(P("obs", "cells", None, None), P("obs", "cells")),
        check_vma=False,
    )
```

profile of v0, /device:TPU:4, one launch (start us, length us, event | category | flops | bytes accessed | tf_op | source)
XLA Modules:
  0.0 554.4 jit_solution(576463983085846463)
XLA Ops:
  8.7 1.7 pad_maximum_fusion
  11.7 3.7 collective-permute-start
  15.4 2.3 collective-permute-start.2
  19.1 2.6 select_maximum_fusion.8
  21.9 1.5 copy-done.1
  23.4 6.8 %select_maximum_fusion.6 = f32[256,3,10,130]{3,2,1,0:T(8,128)S(1)} fusion(f32[256,1,8,128]{3,2,1,0:T(8,128)S(1)} %collective-permute-done.3, f32[256,1,8,128]{3,2,1,0:T(8,128)} %param.8, f32[256,1,8,128]{3,2,1,0:T(8,128)S(1)} %collective-permute-done.2), kind=kLoop, calls=%fused_computation.13 | loop fusion | flops 14976000 | bytes 7139328 | tf_op jit(solution)/shard_map/concatenate | solution.py:23
  32.9 23.3 %collective-permute-start.4 = (f32[256,1,8,128]{3,2,1,0:T(8,128)S(1)}, f32[256,1,8,128]{3,2,1,0:T(8,128)S(1)}, u32[]{:S(2)}, u32[]{:S(2)}) collective-permute-start(f32[256,1,8,128]{3,2,1,0:T(8,128)S(1)} %get-tuple-element.5), channel_id=1, source_target_pairs={{0,1},{1,2},{2,3},{3,4},{4,5},{5,6},{6,7},{7,8},{8,9},{9,10},{10,1... | collective-permute-start | bytes 3145736 | tf_op jit(solution)/shard_map/ppermute | solution.py:19
  56.4 2.1 collective-permute-done.4
  58.4 5.8 %select_maximum_fusion.4 = f32[256,3,10,130]{3,2,1,0:T(8,128)S(1)} fusion(f32[256,1,8,128]{3,2,1,0:T(8,128)S(1)} %collective-permute-done.5, f32[256,1,8,128]{3,2,1,0:T(8,128)S(1)} %get-tuple-element.5, f32[256,1,8,128]{3,2,1,0:T(8,128)S(1)} %collective-permute-done.4), kind=kLoop, calls=%fused_computation.11 | loop fusion | flops 14976000 | bytes 7139328 | tf_op jit(solution)/shard_map/concatenate | solution.py:23
  64.3 1.7 fusion.47
  67.3 20.0 %collective-permute-start.6 = (f32[256,1,8,128]{3,2,1,0:T(8,128)S(1)}, f32[256,1,8,128]{3,2,1,0:T(8,128)S(1)}, u32[]{:S(2)}, u32[]{:S(2)}) collective-permute-start(f32[256,1,8,128]{3,2,1,0:T(8,128)S(1)} %get-tuple-element.3), channel_id=1, source_target_pairs={{0,1},{1,2},{2,3},{3,4},{4,5},{5,6},{6,7},{7,8},{8,9},{9,10},{10,1... | collective-permute-start | bytes 3145736 | tf_op jit(solution)/shard_map/ppermute | solution.py:19
  87.5 2.1 collective-permute-done.6
  89.5 5.8 %select_maximum_fusion.2 = f32[256,3,10,130]{3,2,1,0:T(8,128)S(1)} fusion(f32[256,1,8,128]{3,2,1,0:T(8,128)S(1)} %collective-permute-done.7, f32[256,1,8,128]{3,2,1,0:T(8,128)S(1)} %get-tuple-element.3, f32[256,1,8,128]{3,2,1,0:T(8,128)S(1)} %collective-permute-done.6), kind=kLoop, calls=%fused_computation.9 | loop fusion | flops 14976000 | bytes 7139328 | tf_op jit(solution)/shard_map/concatenate | solution.py:23
  95.4 2.6 fusion.13
  97.9 17.4 %collective-permute-start.9 = (f32[256,1,8,128]{3,2,1,0:T(8,128)}, f32[256,1,8,128]{3,2,1,0:T(8,128)}, u32[]{:S(2)}, u32[]{:S(2)}) collective-permute-start(f32[256,1,8,128]{3,2,1,0:T(8,128)} %fusion.13), channel_id=1, source_target_pairs={{0,1},{1,2},{2,3},{3,4},{4,5},{5,6},{6,7},{7,8},{8,9},{9,10},{10,1... | collective-permute-start | bytes 3145736 | tf_op jit(solution)/shard_map/ppermute | solution.py:19
  115.4 1.5 collective-permute-start.8
  118.9 2.3 fusion.37
  122.3 2.0 gather_fusion.2
  124.3 7.1 %select_maximum_fusion = f32[256,3,10,130]{3,2,1,0:T(8,128)S(1)} fusion(f32[256,1,8,128]{3,2,1,0:T(8,128)} %collective-permute-done.8, f32[256,1,8,128]{3,2,1,0:T(8,128)} %fusion.13, f32[256,1,8,128]{3,2,1,0:T(8,128)} %collective-permute-done.9), kind=kLoop, calls=%fused_computation.7 | loop fusion | flops 14976000 | bytes 7139328 | tf_op jit(solution)/shard_map/concatenate | solution.py:23
  131.4 2.5 fusion.17
  135.4 252.5 %all-gather.2.cloned.1.call-done = f32[4096,1024]{1,0:T(8,128)} async-done(((f32[256,1024]{1,0:T(8,128)}), f32[4096,1024]{1,0:T(8,128)}) %all-gather.2.cloned.1.call-update) | async-done | bytes 16777232 | tf_op jit(solution)/shard_map/all_gather | solution.py:136
  387.8 18.1 %fusion.46 = f32[256,4096]{1,0:T(8,128)} fusion(f32[4096,1024]{1,0:T(8,128)} %all-gather.2.cloned.1.call-done, f32[32,8,8,128]{3,2,1,0:T(8,128)S(1)} %bitcast.47), kind=kOutput, calls=%fused_computation.109 | convolution fusion | flops 12884901888 | bytes 22020096 | tf_op jit(solution)/shard_map/dot_general | solution.py:102
  406.0 139.9 %all-reduce.7.cloned.1.call-done = f32[256,4096]{1,0:T(8,128)} async-done(((f32[256,4096]{1,0:T(8,128)}), f32[256,4096]{1,0:T(8,128)}) %all-reduce.7.cloned.1.call-update) | async-done | bytes 4194320 | tf_op jit(solution)/shard_map/psum | solution.py:138
  545.9 1.7 dynamic-slice_multiply_fusion
  (41 shorter events, 13.0 us)
Async XLA Ops:
  7.2 23.1 %copy-start.3 = (f32[256,1,8,128]{3,2,1,0:T(8,128)S(1)}, f32[256,1,8,128]{3,2,1,0:T(8,128)}, u32[]{:S(2)}) copy-start(f32[256,1,8,128]{3,2,1,0:T(8,128)} %param.8) | copy-start | bytes 3145732
  7.2 23.1 %copy-start.4 = (s32[256]{0:T(256)S(1)}, s32[256]{0:T(256)}, u32[]{:S(2)}) copy-start(s32[256]{0:T(256)} %param.12) | copy-start | bytes 3076
  7.2 380.7 %all-gather.2.cloned.1.call-start = ((), (), s32[]{:S(2)}) async-start(), calls=%async_computation | async-start | bytes 17825792 | tf_op jit(solution)/shard_map/all_gather | solution.py:136
  10.4 8.7 %collective-permute-start.1 = (f32[65,1,8,128]{3,2,1,0:T(8,128)}, f32[65,1,8,128]{3,2,1,0:T(8,128)S(1)}, u32[]{:S(2)}, u32[]{:S(2)}) collective-permute-start(f32[65,1,8,128]{3,2,1,0:T(8,128)} %pad_maximum_fusion), channel_id=1, source_target_pairs={{1,0},{2,1},{3,2},{4,3},{5,4},{6,5},{7,6},{8,7},{9,8},{10,9},{11,1... | collective-permute-start | bytes 798728 | tf_op jit(solution)/shard_map/ppermute | solution.py:22
  11.7 7.4 %collective-permute-start = (f32[65,1,8,128]{3,2,1,0:T(8,128)}, f32[65,1,8,128]{3,2,1,0:T(8,128)}, u32[]{:S(2)}, u32[]{:S(2)}) collective-permute-start(f32[65,1,8,128]{3,2,1,0:T(8,128)} %pad_maximum_fusion), channel_id=1, source_target_pairs={{0,1},{1,2},{2,3},{3,4},{4,5},{5,6},{6,7},{7,8},{8,9},{9,10},{10,1... | collective-permute-start | bytes 798728 | tf_op jit(solution)/shard_map/ppermute | solution.py:19
  15.4 6.4 %collective-permute-start.2 = (f32[256,1,8,128]{3,2,1,0:T(8,128)}, f32[256,1,8,128]{3,2,1,0:T(8,128)S(1)}, u32[]{:S(2)}, u32[]{:S(2)}) collective-permute-start(f32[256,1,8,128]{3,2,1,0:T(8,128)} %param.8), channel_id=1, source_target_pairs={{0,1},{1,2},{2,3},{3,4},{4,5},{5,6},{6,7},{7,8},{8,9},{9,10},{10,1... | collective-permute-start | bytes 3145736 | tf_op jit(solution)/shard_map/ppermute | solution.py:19
  17.8 5.6 %collective-permute-start.3 = (f32[256,1,8,128]{3,2,1,0:T(8,128)}, f32[256,1,8,128]{3,2,1,0:T(8,128)S(1)}, u32[]{:S(2)}, u32[]{:S(2)}) collective-permute-start(f32[256,1,8,128]{3,2,1,0:T(8,128)} %param.8), channel_id=1, source_target_pairs={{1,0},{2,1},{3,2},{4,3},{5,4},{6,5},{7,6},{8,7},{9,8},{10,9},{11,1... | collective-permute-start | bytes 3145736 | tf_op jit(solution)/shard_map/ppermute | solution.py:22
  21.7 1.7 copy-start.1
  31.6 24.8 %collective-permute-start.5 = (f32[256,1,8,128]{3,2,1,0:T(8,128)S(1)}, f32[256,1,8,128]{3,2,1,0:T(8,128)S(1)}, u32[]{:S(2)}, u32[]{:S(2)}) collective-permute-start(f32[256,1,8,128]{3,2,1,0:T(8,128)S(1)} %get-tuple-element.5), channel_id=1, source_target_pairs={{1,0},{2,1},{3,2},{4,3},{5,4},{6,5},{7,6},{8,7},{9,8},{10,9},{11,1... | collective-permute-start | bytes 3145736 | tf_op jit(solution)/shard_map/ppermute | solution.py:22
  32.9 25.5 %collective-permute-start.4 = (f32[256,1,8,128]{3,2,1,0:T(8,128)S(1)}, f32[256,1,8,128]{3,2,1,0:T(8,128)S(1)}, u32[]{:S(2)}, u32[]{:S(2)}) collective-permute-start(f32[256,1,8,128]{3,2,1,0:T(8,128)S(1)} %get-tuple-element.5), channel_id=1, source_target_pairs={{0,1},{1,2},{2,3},{3,4},{4,5},{5,6},{6,7},{7,8},{8,9},{9,10},{10,1... | collective-permute-start | bytes 3145736 | tf_op jit(solution)/shard_map/ppermute | solution.py:19
  66.0 21.5 %collective-permute-start.7 = (f32[256,1,8,128]{3,2,1,0:T(8,128)S(1)}, f32[256,1,8,128]{3,2,1,0:T(8,128)S(1)}, u32[]{:S(2)}, u32[]{:S(2)}) collective-permute-start(f32[256,1,8,128]{3,2,1,0:T(8,128)S(1)} %get-tuple-element.3), channel_id=1, source_target_pairs={{1,0},{2,1},{3,2},{4,3},{5,4},{6,5},{7,6},{8,7},{9,8},{10,9},{11,1... | collective-permute-start | bytes 3145736 | tf_op jit(solution)/shard_map/ppermute | solution.py:22
  67.3 22.2 %collective-permute-start.6 = (f32[256,1,8,128]{3,2,1,0:T(8,128)S(1)}, f32[256,1,8,128]{3,2,1,0:T(8,128)S(1)}, u32[]{:S(2)}, u32[]{:S(2)}) collective-permute-start(f32[256,1,8,128]{3,2,1,0:T(8,128)S(1)} %get-tuple-element.3), channel_id=1, source_target_pairs={{0,1},{1,2},{2,3},{3,4},{4,5},{5,6},{6,7},{7,8},{8,9},{9,10},{10,1... | collective-permute-start | bytes 3145736 | tf_op jit(solution)/shard_map/ppermute | solution.py:19
  87.3 29.5 %copy-start.5 = (s32[256]{0:T(256)S(1)}, s32[256]{0:T(256)}, u32[]{:S(2)}) copy-start(s32[256]{0:T(256)} %param.13) | copy-start | bytes 3076
  97.9 26.4 %collective-permute-start.9 = (f32[256,1,8,128]{3,2,1,0:T(8,128)}, f32[256,1,8,128]{3,2,1,0:T(8,128)}, u32[]{:S(2)}, u32[]{:S(2)}) collective-permute-start(f32[256,1,8,128]{3,2,1,0:T(8,128)} %fusion.13), channel_id=1, source_target_pairs={{0,1},{1,2},{2,3},{3,4},{4,5},{5,6},{6,7},{7,8},{8,9},{9,10},{10,1... | collective-permute-start | bytes 3145736 | tf_op jit(solution)/shard_map/ppermute | solution.py:19
  115.4 8.9 %collective-permute-start.8 = (f32[256,1,8,128]{3,2,1,0:T(8,128)}, f32[256,1,8,128]{3,2,1,0:T(8,128)}, u32[]{:S(2)}, u32[]{:S(2)}) collective-permute-start(f32[256,1,8,128]{3,2,1,0:T(8,128)} %fusion.13), channel_id=1, source_target_pairs={{1,0},{2,1},{3,2},{4,3},{5,4},{6,5},{7,6},{8,7},{9,8},{10,9},{11,1... | collective-permute-start | bytes 3145736 | tf_op jit(solution)/shard_map/ppermute | solution.py:22
  124.3 7.1 %copy-start.2 = (f32[256,8,128]{2,1,0:T(8,128)S(1)}, f32[256,8,128]{2,1,0:T(8,128)}, u32[]{:S(2)}) copy-start(f32[256,8,128]{2,1,0:T(8,128)} %gather_fusion.2) | copy-start | bytes 3145732
  133.9 272.0 %copy-start = (f32[256,1,8,128]{3,2,1,0:T(8,128)}, f32[256,1,8,128]{3,2,1,0:T(8,128)S(1)}, u32[]{:S(2)}) copy-start(f32[256,1,8,128]{3,2,1,0:T(8,128)S(1)} %fusion.17) | copy-start | bytes 3145732
  135.3 410.6 %all-reduce.7.cloned.1.call-start = ((), (), s32[]{:S(2)}) async-start(), calls=%async_computation.1 | async-start | bytes 8388608 | tf_op jit(solution)/shard_map/psum | solution.py:138
Sparse Core Ops, SparseCore 0:
  135.4 252.3 all-gather.1
  406.1 139.7 all-reduce.6
where the time goes:
time: 555 us; the launch traced here: 554 us
  waiting for transfers between devices  397 us (72%)
  starting transfers between devices  73.5 us (13%)
  other arithmetic  43.9 us (8%)
  matrix products  18.1 us (3%)
  between operations  14.4 us (3%)
  local copies, waits for them, and re-layouts  7.7 us (1%)
    all_gather x1, waiting for transfers between devices, per_device(): lax.all_gather(panel, 'obs', axis=0, tiled=True)  252 us
    psum x1, waiting for transfers between devices, per_device(): summed = lax.psum(partial_value, 'cells')  140 us
    ppermute x5, starting transfers between devices, with_halo(): lax.ppermute(lax.slice_in_dim(block, block.shape[dim] - width, None, axis...  66.8 us
    concatenate x5, other arithmetic, with_halo(): block = jnp.concatenate([low, block, high], axis=dim)  28.1 us
    dot_general x1, matrix products, product_rows(): lax.dot_general(left, right, (((1,), (1,)), ((), ())), preferred_element_...  18.1 us
  transfers between devices with their start and end apart: 12, of which 6 were waited for; matrix products, arithmetic and copies ran while one was open for 2% of the time, Pallas kernels for 0%

commit v1 on v0

v1 whole, which is shorter than its diff:
```python
import jax
import jax.numpy as jnp
from jax import lax
from jax.experimental import pallas as pl
from jax.experimental.pallas import tpu as pltpu
from jax.sharding import PartitionSpec as P

SWEEPS = 3
SOURCE = 16.0
CENTRE = 1.075
HALFWIDTH = 0.925

OBS_AXES = ("z", "xh")
CELL_AXES = ("y", "xl", "core")
PLANE = ("xh", "y", "xl")
LAYERS = 16
GROUP = 16
ROWS = 256
TESTS = 64
NY, NZ = 8, 128
F32, BF16 = jnp.float32, jnp.bfloat16

VMEM = pl.BlockSpec(memory_space=pltpu.VMEM)
SMEM = pl.BlockSpec(memory_space=pltpu.SMEM)


def call(kernel, outs, specs, scratch=(), flops=0, moved=0):
    return pl.pallas_call(
        kernel,
        out_shape=outs,
        in_specs=specs,
        out_specs=jax.tree.map(lambda _: VMEM, outs),
        scratch_shapes=list(scratch),
        compiler_params=pltpu.CompilerParams(vmem_limit_bytes=40 * 2**20),
        cost_estimate=pl.CostEstimate(flops=flops, bytes_accessed=moved, transcendentals=0),
    )


def shape(*dims, dtype=F32):
    return jax.ShapeDtypeStruct(dims, dtype)


def places():
    row = lax.broadcasted_iota(jnp.int32, (NY, NZ), 0)
    col = lax.broadcasted_iota(jnp.int32, (NY, NZ), 1)
    return row, col


def beside(v):
    return (
        pltpu.roll(v, 1, 0),
        pltpu.roll(v, NY - 1, 0),
        pltpu.roll(v, 1, 1),
        pltpu.roll(v, NZ - 1, 1),
    )


def inside():
    row, col = places()
    return (row > 0, row < NY - 1, col > 0, col < NZ - 1)


def pack_kernel(logk_ref, label_ref, start_ref, packed_ref, conduct_ref):
    label = label_ref[0]
    logk = jnp.zeros((NY, NZ), F32)
    for zone in range(logk_ref.shape[0]):
        logk = jnp.where(label == zone, logk_ref[zone], logk)
    conduct = jnp.exp(logk)
    conduct_ref[...] = conduct
    for target in range(LAYERS):
        packed_ref[target, 0:GROUP] = start_ref[target]
        packed_ref[target, GROUP] = conduct


def sweep_kernel(me_ref, cell_ref, got_ref, out_ref, weight_ref, source_ref):
    row, col = places()
    flat = row * NZ + col
    inner = inside()

    def face(a, b):
        return 2.0 * a * b / (a + b)

    below = None
    for layer in range(LAYERS):
        here = got_ref[layer, GROUP]
        above = face(here, got_ref[layer + 1, GROUP]) if layer + 1 < LAYERS else None
        edge = [face(here, b) for b in beside(here)]
        faces = [here if below is None else below, here if above is None else above]
        faces += [jnp.where(ok, w, here) for ok, w in zip(inner, edge)]
        diagonal = faces[0]
        for extra in faces[1:]:
            diagonal = diagonal + extra
        inverse = 1.0 / diagonal
        if below is not None:
            weight_ref[layer, 0] = below * inverse
        if above is not None:
            weight_ref[layer, 1] = above * inverse
        for i, (ok, w) in enumerate(zip(inner, edge)):
            weight_ref[layer, 2 + i] = jnp.where(ok, w, 0.0) * inverse
        weight_ref[layer, 6] = inverse
        source_ref[layer] = jnp.zeros((NY, NZ), F32)
        below = above

    ratio = CENTRE / HALFWIDTH
    first = me_ref[0] * GROUP

    def one(k, carry):
        cell = cell_ref[first + k]
        layer_of = cell // (NY * NZ)
        hit = flat == cell - layer_of * (NY * NZ)
        source_ref[layer_of] = jnp.where(hit, SOURCE * weight_ref[layer_of, 6], 0.0)
        v = [got_ref[layer, k] for layer in range(LAYERS)]
        update = None
        damping = 1.0 / ratio
        for sweep in range(SWEEPS):
            misfit = []
            for layer in range(LAYERS):
                m = source_ref[layer] - v[layer]
                if layer > 0:
                    m = m + weight_ref[layer, 0] * v[layer - 1]
                if layer + 1 < LAYERS:
                    m = m + weight_ref[layer, 1] * v[layer + 1]
                for i, b in enumerate(beside(v[layer])):
                    m = m + weight_ref[layer, 2 + i] * b
                misfit.append(m)
            if sweep == 0:
                update = [m * (1.0 / CENTRE) for m in misfit]
            else:
                newer = 1.0 / (2.0 * ratio - damping)
                keep, add = newer * damping, 2.0 * newer / HALFWIDTH
                update = [keep * u + add * m for u, m in zip(update, misfit)]
                damping = newer
            v = [a + u for a, u in zip(v, update)]
        for layer in range(LAYERS):
            out_ref[layer, k, 0] = v[layer]
            if layer == 0:
                slope = v[1]
            elif layer + 1 == LAYERS:
                slope = -v[layer - 1]
            else:
                slope = v[layer + 1] - v[layer - 1]
            out_ref[layer, k, 1] = slope * 0.5
        source_ref[layer_of] = jnp.zeros((NY, NZ), F32)
        return carry

    lax.fori_loop(0, GROUP, one, 0)


def sensitivity_kernel(
    me_ref, test_ref, conduct_ref, heads_ref, low_ref, high_ref, field_ref,
    sens_ref, keep_ref, send_ref, slope_ref,
):
    ok = [jnp.where(o, 0.5, 0.0).astype(F32) for o in inside()]

    def along_y(v):
        return ok[1] * pltpu.roll(v, NY - 1, 0) - ok[0] * pltpu.roll(v, 1, 0)

    def along_z(v):
        return ok[3] * pltpu.roll(v, NZ - 1, 1) - ok[2] * pltpu.roll(v, 1, 1)

    factor = -conduct_ref[...]

    def slopes(t, carry):
        h = heads_ref[t]
        slope_ref[t, 0] = factor * ((high_ref[t] - low_ref[t]) * 0.5)
        slope_ref[t, 1] = factor * along_y(h)
        slope_ref[t, 2] = factor * along_z(h)
        return carry

    lax.fori_loop(0, TESTS, slopes, 0, unroll=4)
    mine = me_ref[1]

    def eight(block, carry):
        for i in range(8):
            k = block * 8 + i
            t = test_ref[k]
            v = field_ref[k, 0]
            total = field_ref[k, 1] * slope_ref[t, 0]
            total = total + along_y(v) * slope_ref[t, 1]
            total = total + along_z(v) * slope_ref[t, 2]
            sens_ref[pl.ds(pl.multiple_of(k * NY, NY), NY), :] = total
        here = pl.ds(pl.multiple_of(block * 8, 8), 8)
        for i in range(NY // 2):
            at = block * 64 + i
            lanes = pl.ds(i * NZ, NZ)
            keep_ref[here, lanes] = sens_ref[pl.ds(at + mine * (NY // 2), 8, stride=NY), :]
            send_ref[here, lanes] = sens_ref[pl.ds(at + (1 - mine) * (NY // 2), 8, stride=NY), :]
        return carry

    lax.fori_loop(0, ROWS // 8, eight, 0)


def split_into(ref, high_ref, low_ref, at, which):
    x = ref[...]
    high = x.astype(BF16)
    high_ref[at, which] = high
    low_ref[at, which] = (x - high.astype(F32)).astype(BF16)


def product(high_ref, low_ref, left, right):
    def dot(a, b):
        return lax.dot_general(a, b, (((1,), (1,)), ((), ())), preferred_element_type=F32)

    lh, ll = high_ref[left], low_ref[left]
    rh, rl = high_ref[right], low_ref[right]
    return dot(lh, rh) + (dot(lh, rl) + dot(ll, rh))


def near_kernel(me_ref, a0, b0, a1, b1, am, bm, mine_ref, theirs_ref, high_ref, low_ref):
    for at, pair in enumerate(((a0, b0), (a1, b1), (am, bm))):
        for which, ref in enumerate(pair):
            split_into(ref, high_ref, low_ref, at, which)
    xh, core = me_ref[1], me_ref[2]
    for side, out_ref in enumerate((mine_ref, theirs_ref)):
        right = side ^ core ^ xh
        for d, (a, b) in enumerate(((0, 0), (0, 1), (2, 1))):
            for half in range(2):
                block = product(high_ref, low_ref, (a, half ^ xh), (b, right))
                out_ref[:, 2 * d + half] = block.reshape(16, 16, ROWS)


def far_kernel(me_ref, am, bm, a2, b2, an, bn, mine_ref, theirs_ref, high_ref, low_ref):
    for at, pair in enumerate(((am, bm), (a2, b2), (an, bn))):
        for which, ref in enumerate(pair):
            split_into(ref, high_ref, low_ref, at, which)
    xh, core, late = me_ref[1], me_ref[2], me_ref[4]
    for side, out_ref in enumerate((mine_ref, theirs_ref)):
        right = side ^ core ^ xh
        for half in range(2):
            block = product(high_ref, low_ref, (0, half ^ xh), (1, right))
            out_ref[:, half] = block.reshape(16, 16, ROWS)
        block = product(high_ref, low_ref, (1 + late, late ^ xh), (2 - late, right))
        out_ref[:, 2] = block.reshape(16, 16, ROWS)


def total_kernel(parts_ref, out_ref):
    total = parts_ref[0]
    for i in range(1, parts_ref.shape[0]):
        total = total + parts_ref[i]
    out_ref[...] = total


def opposite(me_ref, up2, down2):
    first = me_ref[5] == 1
    return jnp.where(first, up2[2], down2[0]), jnp.where(first, down2[0], up2[2])


def give_kernel(me_ref, up1, up2, down2, give_ref):
    other = 1 - me_ref[2]
    give_ref[0] = up1[other]
    give_ref[1] = up1[2 + other]
    give_ref[2] = up2[other]
    pair = opposite(me_ref, up2, down2)
    give_ref[3] = jnp.where(other == 0, pair[0], pair[1])


def place_kernel(me_ref, near, up1, down1, up2, down2, got, slot_ref):
    core, z, first = me_ref[2], me_ref[3], me_ref[5]
    for r in range(4):
        for half in range(2):
            source = near[2 * r + half] if r < 2 else down1[2 * (r - 2) + half]
            slot_ref[half, (z + r) % 8] = source
    for i, (r, ref, at) in enumerate(((7, up1, 0), (6, up1, 2), (5, up2, 0))):
        slot_ref[core, (z + r) % 8] = ref[at + core]
        slot_ref[1 - core, (z + r) % 8] = got[i]
    pair = opposite(me_ref, up2, down2)
    own = jnp.where(core == 0, pair[0], pair[1])
    mine = jnp.where(first == 1, jnp.where(core == 0, pair[0], pair[1]), own)
    others = jnp.where(first == 1, jnp.where(core == 0, pair[1], pair[0]), got[3])
    slot_ref[core, (z + 4) % 8] = mine
    slot_ref[1 - core, (z + 4) % 8] = others


def finish_kernel(me_ref, block_ref, out_ref):
    flip = me_ref[6] == 1
    scale = 1.0 / (LAYERS * NY * NZ)

    @pl.when(flip)
    def _():
        out_ref[...] = block_ref[...].T * scale

    @pl.when(jnp.logical_not(flip))
    def _():
        out_ref[...] = block_ref[...] * scale


def swap(x, axis):
    return lax.ppermute(x, axis, [(0, 1), (1, 0)])


def round_z(x, by):
    return lax.ppermute(x, "z", [(i, (i + by) % 8) for i in range(8)])


def per_device(adjoint_start, forward_heads, zone_label, zone_logk, obs_cell, test_of_obs):
    cells = lax.axis_index(CELL_AXES)
    xh, core, z = lax.axis_index("xh"), lax.axis_index("core"), lax.axis_index("z")
    z2 = lax.axis_index(("y", "xl"))
    late = (z >= 4).astype(jnp.int32)
    first = ((z >= 2) & (z < 6)).astype(jnp.int32)
    r = (z2 - z + 8) % 8
    flip = ((r >= 5) | ((r == 4) & (first == 0))).astype(jnp.int32)
    me = jnp.stack([cells, xh, core, z, late, first, flip, flip]).astype(jnp.int32)

    heads = forward_heads.reshape(TESTS, NY, NZ)
    low = lax.ppermute(heads, CELL_AXES, [(i, i + 1) for i in range(LAYERS - 1)])
    high = lax.ppermute(heads, CELL_AXES, [(i + 1, i) for i in range(LAYERS - 1)])

    packed, conduct = call(
        pack_kernel,
        (shape(LAYERS, GROUP + 1, NY, NZ), shape(NY, NZ)),
        [SMEM, VMEM, VMEM],
    )(zone_logk, zone_label, adjoint_start.reshape(LAYERS, GROUP, NY, NZ))
    got = lax.all_to_all(packed, CELL_AXES, 0, 0, tiled=True)
    swept = call(
        sweep_kernel,
        shape(LAYERS, GROUP, 2, NY, NZ),
        [SMEM, SMEM, VMEM],
        [pltpu.VMEM((LAYERS, 7, NY, NZ), F32), pltpu.VMEM((LAYERS, NY, NZ), F32)],
    )(me, obs_cell, got)
    field = lax.all_to_all(swept, CELL_AXES, 0, 0, tiled=True).reshape(ROWS, 2, NY, NZ)

    half = NY * NZ // 2
    sens, a0, send = call(
        sensitivity_kernel,
        (shape(ROWS * NY, NZ), shape(ROWS, half), shape(ROWS, half)),
        [SMEM, SMEM, VMEM, VMEM, VMEM, VMEM, VMEM],
        [pltpu.VMEM((TESTS, 3, NY, NZ), F32)],
    )(me, test_of_obs, conduct, heads, low, high, field)

    a1, am = round_z(a0, -1), round_z(a0, 1)
    b0 = swap(send, "xh")
    b1, bm = round_z(b0, -1), round_z(b0, 1)
    a2, an = round_z(a1, -1), round_z(am, 1)
    b2, bn = round_z(b1, -1), round_z(bm, 1)

    def partial(kernel, count, *blocks):
        scratch = [pltpu.VMEM((3, 2, ROWS, half), BF16)] * 2
        out = shape(16, count, 16, ROWS)
        mine, theirs = call(
            kernel, (out, out), [SMEM] + [VMEM] * 6, scratch,
            flops=2 * 6 * count * ROWS * ROWS * half, moved=2**23,
        )(me, *blocks)
        both = mine + swap(theirs, "core")
        parts = lax.all_to_all(both, PLANE, 0, 0, tiled=True)
        return call(total_kernel, shape(count, 16, ROWS), [VMEM])(parts)

    near = partial(near_kernel, 6, a0, b0, a1, b1, am, bm)
    far = partial(far_kernel, 3, am, bm, a2, b2, an, bn)

    up1 = round_z(near[2:6], 1)
    down1 = round_z(jnp.concatenate([near[4:6], far[0:2]]), -1)
    up2 = round_z(far, 2)
    down2 = round_z(far[2:3], -2)
    give = call(give_kernel, shape(4, 16, ROWS), [SMEM] + [VMEM] * 3)(me, up1, up2, down2)
    swapped = swap(give, "core")
    slots = call(place_kernel, shape(2, 8, 16, ROWS), [SMEM] + [VMEM] * 6)(
        me, near, up1, down1, up2, down2, swapped
    )
    block = lax.all_to_all(slots.reshape(16, 16, ROWS), PLANE, 0, 0, tiled=True)
    gram = call(finish_kernel, shape(ROWS, ROWS), [SMEM, VMEM])(me, block.reshape(ROWS, ROWS))
    return sens.reshape(ROWS, 1, NY, NZ), gram


def solution(mesh):
    fine = jax.sharding.Mesh(
        mesh.devices.reshape(8, 2, 4, 2, 2), ("z", "xh", "y", "xl", "core")
    )
    return jax.shard_map(
        per_device,
        mesh=fine,
        in_specs=(
            P(OBS_AXES, CELL_AXES, None, None),
            P(None, CELL_AXES, None, None),
            P(CELL_AXES, None, None),
            P(),
            P(OBS_AXES),
            P(OBS_AXES),
        ),
        out_specs=(P(OBS_AXES, CELL_AXES, None, None), P(OBS_AXES, CELL_AXES)),
        check_vma=False,
    )
```

time: 555 us -> 213 us (0.38)
  waiting for transfers between devices: 397 us -> 99.5 us
  other arithmetic: 43.9 us -> 3.92 us
  Pallas kernels: 0 us -> 24.4 us
  matrix products: 18.1 us -> 0 us
  blocking collectives: 0 us -> 14.1 us
  between operations: 14.4 us -> 0.86 us
  starting transfers between devices: 73.5 us -> 65.5 us
    all_gather x1 -> x0, waiting for transfers between devices: 252 us -> none  [per_device(): lax.all_gather(panel, 'obs', axis=0, tiled=True)]
    psum x1 -> x0, waiting for transfers between devices: 140 us -> none  [per_device(): summed = lax.psum(partial_value, 'cells')]
    all_to_all x0 -> x4, waiting for transfers between devices: none -> 64.3 us  [the longest x2 26 us: partial(): parts = lax.all_to_all(both, PLANE, 0, 0, tiled=True)]
    ppermute x10 -> x18, starting transfers between devices: 73.5 us -> 36.7 us  [the longest x12 26.2 us: round_z(): return lax.ppermute(x, 'z', [(i, (i + by) % 8) for i in range(8)])]
    ppermute x10 -> x18, waiting for transfers between devices: 4.4 us -> 35.2 us  [the longest x12 22.5 us: round_z(): return lax.ppermute(x, 'z', [(i, (i + by) % 8) for i in range(8)])]
    concatenate x6 -> x1, other arithmetic: 29.8 us -> 0.01 us  [per_device(): down1 = round_z(jnp.concatenate([near[4:6], far[0:2]]), -1)]
    all_to_all x0 -> x4, starting transfers between devices: none -> 28.8 us  [the longest x2 19.8 us: partial(): parts = lax.all_to_all(both, PLANE, 0, 0, tiled=True)]
    pallas_call x0 -> x10, Pallas kernels: none -> 24.4 us  [the longest x2 7.65 us: partial(): call(kernel, (out, out), [SMEM] + [VMEM] * 6, scratch, flops=2 * 6 * coun...]
  transfers between devices with their start and end apart: 12 -> 22, of which waited for: 6 -> 14; matrix products, arithmetic and copies ran while one was open for 2% -> 2% of each run, Pallas kernels for 0% -> 4%
where the time goes in v1:
time: 213 us; the launch traced here: 211 us
  waiting for transfers between devices  99.5 us (47%)
  starting transfers between devices  65.5 us (31%)
  Pallas kernels  24.4 us (11%)
  blocking collectives  14.1 us (7%)
  other arithmetic  3.92 us (2%)
  local copies, waits for them, and re-layouts  2.67 us (1%)
    ppermute x12, starting transfers between devices, round_z(): return lax.ppermute(x, 'z', [(i, (i + by) % 8) for i in range(8)])  26.2 us
    all_to_all x2, waiting for transfers between devices, partial(): parts = lax.all_to_all(both, PLANE, 0, 0, tiled=True)  26 us
    ppermute x12, waiting for transfers between devices, round_z(): return lax.ppermute(x, 'z', [(i, (i + by) % 8) for i in range(8)])  22.5 us
    all_to_all x1, waiting for transfers between devices, per_device(): lax.all_to_all(swept, CELL_AXES, 0, 0, tiled=True).reshape(ROWS, 2, NY, NZ)  21.1 us
    all_to_all x2, starting transfers between devices, partial(): parts = lax.all_to_all(both, PLANE, 0, 0, tiled=True)  19.8 us
    all_to_all x1, waiting for transfers between devices, per_device(): got = lax.all_to_all(packed, CELL_AXES, 0, 0, tiled=True)  17.2 us
    all_to_all x1, blocking collectives, per_device(): block = lax.all_to_all(slots.reshape(16, 16, ROWS), PLANE, 0, 0, tiled=True)  14.1 us
    ppermute x4, waiting for transfers between devices, swap(): return lax.ppermute(x, axis, [(0, 1), (1, 0)])  9.41 us
  transfers between devices with their start and end apart: 22, of which 14 were waited for; matrix products, arithmetic and copies ran while one was open for 2% of the time, Pallas kernels for 4%

profile of v1, /device:TPU:4, one launch (start us, length us, event | category | flops | bytes accessed | tf_op | source)
XLA Modules:
  0.0 210.9 jit_solution(11845720118721496379)
XLA Ops:
  4.8 5.2 %all-to-all-start = ((f32[16,17,8,128]{3,2,1,0:T(8,128)}), f32[16,17,8,128]{3,2,1,0:T(8,128)S(1)}, u32[]{:S(2)}, u32[]{:S(2)}) async-start(f32[16,17,8,128]{3,2,1,0:T(8,128)} %get-tuple-element.12), calls=%async_computation | async-start | bytes 2228224 | tf_op jit(solution)/shard_map/all_to_all | solution.py:314
  10.2 17.2 %all-to-all-done.got_ref = f32[16,17,8,128]{3,2,1,0:T(8,128)S(1)} async-done(((f32[16,17,8,128]{3,2,1,0:T(8,128)}), f32[16,17,8,128]{3,2,1,0:T(8,128)S(1)}, u32[]{:S(2)}, u32[]{:S(2)}) %all-to-all-start) | async-done | bytes 1114144 | tf_op jit(solution)/shard_map/all_to_all | solution.py:314
  27.4 6.7 %shard_map.78 = f32[16,16,2,8,128]{4,3,2,1,0:T(8,128)} custom-call(s32[8]{0:T(128)S(1)} %stack.40.me_ref, s32[256]{0:T(256)S(1)} %copy-done.3, f32[16,17,8,128]{3,2,1,0:T(8,128)S(1)} %all-to-all-done.got_ref), custom_call_target="tpu_custom_call" | custom-call | tf_op jit(solution)/shard_map/pallas_call | solution.py:315
  34.1 3.8 %all-to-all-start.1 = ((f32[16,16,2,8,128]{4,3,2,1,0:T(8,128)}), f32[16,16,2,8,128]{4,3,2,1,0:T(8,128)S(1)}, u32[]{:S(2)}, u32[]{:S(2)}) async-start(f32[16,16,2,8,128]{4,3,2,1,0:T(8,128)} %shard_map.78), calls=%async_computation.1 | async-start | bytes 4194304 | tf_op jit(solution)/shard_map/all_to_all | solution.py:321
  41.5 3.2 %collective-permute-done.1.high_ref = f32[64,8,128]{2,1,0:T(8,128)S(1)} collective-permute-done((f32[64,8,128]{2,1,0:T(8,128)S(1)}, f32[64,8,128]{2,1,0:T(8,128)S(1)}, u32[]{:S(2)}, u32[]{:S(2)}) %collective-permute-start.1) | collective-permute-done | bytes 262176 | tf_op jit(solution)/shard_map/ppermute | solution.py:307
  44.7 21.1 %all-to-all-done.1 = f32[16,16,2,8,128]{4,3,2,1,0:T(8,128)S(1)} async-done(((f32[16,16,2,8,128]{4,3,2,1,0:T(8,128)}), f32[16,16,2,8,128]{4,3,2,1,0:T(8,128)S(1)}, u32[]{:S(2)}, u32[]{:S(2)}) %all-to-all-start.1) | async-done | bytes 2097184 | tf_op jit(solution)/shard_map/all_to_all | solution.py:321
  65.8 6.0 %shard_map.79 = (f32[2048,128]{1,0:T(8,128)}, f32[256,512]{1,0:T(8,128)S(1)}, f32[256,512]{1,0:T(8,128)S(1)}) custom-call(s32[8]{0:T(128)S(1)} %stack.40.me_ref, s32[256]{0:T(256)S(1)} %copy-done.4, f32[8,128]{1,0:T(8,128)S(1)} %get-tuple-element.11.conduct_ref, f32[64,8,128]{2,1,0:T(8,128)S(1)} %bitcast.21, f32[64,8,128]{2,1,0:T(8,128)S(1)} %collective-permute-done.low_ref, ...), custom_call_target="tpu_custom_call" | custom-call | tf_op jit(solution)/shard_map/pallas_call | solution.py:324
  74.5 3.9 %collective-permute-start.3 = (f32[256,512]{1,0:T(8,128)S(1)}, f32[256,512]{1,0:T(8,128)S(1)}, u32[]{:S(2)}, u32[]{:S(2)}) collective-permute-start(f32[256,512]{1,0:T(8,128)S(1)} %get-tuple-element.14.a0), channel_id=1, source_target_pairs={{0,224},{32,0},{64,32},{96,64},{128,96},{160,128},{192,160},{224,1... | collective-permute-start | bytes 1572872 | tf_op jit(solution)/shard_map/ppermute | solution.py:292
  78.4 6.3 %collective-permute-done.2.b0 = f32[256,512]{1,0:T(8,128)S(1)} collective-permute-done((f32[256,512]{1,0:T(8,128)S(1)}, f32[256,512]{1,0:T(8,128)S(1)}, u32[]{:S(2)}, u32[]{:S(2)}) %collective-permute-start.2) | collective-permute-done | bytes 524320 | tf_op jit(solution)/shard_map/ppermute | solution.py:288
  84.7 5.9 %collective-permute-start.4 = (f32[256,512]{1,0:T(8,128)S(1)}, f32[256,512]{1,0:T(8,128)S(1)}, u32[]{:S(2)}, u32[]{:S(2)}) collective-permute-start(f32[256,512]{1,0:T(8,128)S(1)} %collective-permute-done.2.b0), channel_id=1, source_target_pairs={{0,224},{32,0},{64,32},{96,64},{128,96},{160,128},{192,160},{224,1... | collective-permute-start | bytes 1572872 | tf_op jit(solution)/shard_map/ppermute | solution.py:292
  90.5 3.3 %collective-permute-start.9 = (f32[256,512]{1,0:T(8,128)S(1)}, f32[256,512]{1,0:T(8,128)S(1)}, u32[]{:S(2)}, u32[]{:S(2)}) collective-permute-start(f32[256,512]{1,0:T(8,128)S(1)} %collective-permute-done.3.a1), channel_id=1, source_target_pairs={{0,224},{32,0},{64,32},{96,64},{128,96},{160,128},{192,160},{224,1... | collective-permute-start | bytes 1572872 | tf_op jit(solution)/shard_map/ppermute | solution.py:292
  93.8 6.7 %collective-permute-done.4.b1 = f32[256,512]{1,0:T(8,128)S(1)} collective-permute-done((f32[256,512]{1,0:T(8,128)S(1)}, f32[256,512]{1,0:T(8,128)S(1)}, u32[]{:S(2)}, u32[]{:S(2)}) %collective-permute-start.4) | collective-permute-done | bytes 524320 | tf_op jit(solution)/shard_map/ppermute | solution.py:292
  100.5 3.7 %collective-permute-start.10 = (f32[256,512]{1,0:T(8,128)S(1)}, f32[256,512]{1,0:T(8,128)S(1)}, u32[]{:S(2)}, u32[]{:S(2)}) collective-permute-start(f32[256,512]{1,0:T(8,128)S(1)} %collective-permute-done.4.b1), channel_id=1, source_target_pairs={{0,224},{32,0},{64,32},{96,64},{128,96},{160,128},{192,160},{224,1... | collective-permute-start | bytes 1572872 | tf_op jit(solution)/shard_map/ppermute | solution.py:292
  104.5 5.0 %shard_map.80 = (f32[16,6,16,256]{3,2,1,0:T(8,128)S(1)}, f32[16,6,16,256]{3,2,1,0:T(8,128)}) custom-call(s32[8]{0:T(128)S(1)} %stack.40.me_ref, f32[256,512]{1,0:T(8,128)S(1)} %get-tuple-element.14.a0, f32[256,512]{1,0:T(8,128)S(1)} %collective-permute-done.2.b0, f32[256,512]{1,0:T(8,128)S(1)} %collective-permute-done.3.a1, ...), custom_call_target="tpu_custom_call" | custom-call | flops 2415919104 | bytes 8388608 | tf_op jit(solution)/shard_map/pallas_call | solution.py:340
  109.5 4.2 %collective-permute-start.7 = (f32[16,6,16,256]{3,2,1,0:T(8,128)}, f32[16,6,16,256]{3,2,1,0:T(8,128)}, u32[]{:S(2)}, u32[]{:S(2)}) collective-permute-start(f32[16,6,16,256]{3,2,1,0:T(8,128)} %get-tuple-element.17), channel_id=1, source_target_pairs={{0,1},{1,0},{2,3},{3,2},{4,5},{5,4},{6,7},{7,6},{8,9},{9,8},{10,11... | collective-permute-start | bytes 4718600 | tf_op jit(solution)/shard_map/ppermute | solution.py:288
  115.7 7.3 %collective-permute-done.10.b2 = f32[256,512]{1,0:T(8,128)S(1)} collective-permute-done((f32[256,512]{1,0:T(8,128)S(1)}, f32[256,512]{1,0:T(8,128)S(1)}, u32[]{:S(2)}, u32[]{:S(2)}) %collective-permute-start.10) | collective-permute-done | bytes 524320 | tf_op jit(solution)/shard_map/ppermute | solution.py:292
  123.0 4.0 %collective-permute-done.12.bn = f32[256,512]{1,0:T(8,128)S(1)} collective-permute-done((f32[256,512]{1,0:T(8,128)S(1)}, f32[256,512]{1,0:T(8,128)S(1)}, u32[]{:S(2)}, u32[]{:S(2)}) %collective-permute-start.12) | collective-permute-done | bytes 524320 | tf_op jit(solution)/shard_map/ppermute | solution.py:292
  134.5 13.0 %all-to-all-start.3 = ((f32[16,3,16,256]{3,2,1,0:T(8,128)}), f32[16,3,16,256]{3,2,1,0:T(8,128)S(1)}, u32[]{:S(2)}, u32[]{:S(2)}) async-start(f32[16,3,16,256]{3,2,1,0:T(8,128)} %add.28), calls=%async_computation.3 | async-start | bytes 1572864 | tf_op jit(solution)/shard_map/all_to_all | solution.py:345
  150.4 9.2 %all-to-all-done.3.parts_ref = f32[16,3,16,256]{3,2,1,0:T(8,128)S(1)} async-done(((f32[16,3,16,256]{3,2,1,0:T(8,128)}), f32[16,3,16,256]{3,2,1,0:T(8,128)S(1)}, u32[]{:S(2)}, u32[]{:S(2)}) %all-to-all-start.3) | async-done | bytes 786464 | tf_op jit(solution)/shard_map/all_to_all | solution.py:345
  159.6 6.7 %all-to-all-start.2 = ((f32[16,6,16,256]{3,2,1,0:T(8,128)}), f32[16,6,16,256]{3,2,1,0:T(8,128)S(1)}, u32[]{:S(2)}, u32[]{:S(2)}) async-start(f32[16,6,16,256]{3,2,1,0:T(8,128)} %add.27), calls=%async_computation.2 | async-start | bytes 3145728 | tf_op jit(solution)/shard_map/all_to_all | solution.py:345
  166.5 4.1 %collective-permute-start.16 = (f32[1,16,256]{2,1,0:T(8,128)S(1)}, f32[1,16,256]{2,1,0:T(8,128)S(1)}, u32[]{:S(2)}, u32[]{:S(2)}) collective-permute-start(f32[1,16,256]{2,1,0:T(8,128)S(1)} %slice.19), channel_id=1, source_target_pairs={{0,192},{32,224},{64,0},{96,32},{128,64},{160,96},{192,128},{224,1... | collective-permute-start | bytes 49160 | tf_op jit(solution)/shard_map/ppermute | solution.py:292
  170.6 16.8 %all-to-all-done.2.parts_ref = f32[16,6,16,256]{3,2,1,0:T(8,128)S(1)} async-done(((f32[16,6,16,256]{3,2,1,0:T(8,128)}), f32[16,6,16,256]{3,2,1,0:T(8,128)S(1)}, u32[]{:S(2)}, u32[]{:S(2)}) %all-to-all-start.2) | async-done | bytes 1572896 | tf_op jit(solution)/shard_map/all_to_all | solution.py:345
  187.6 3.2 %collective-permute-start.14 = (f32[4,16,256]{2,1,0:T(8,128)S(1)}, f32[4,16,256]{2,1,0:T(8,128)S(1)}, u32[]{:S(2)}, u32[]{:S(2)}) collective-permute-start(f32[4,16,256]{2,1,0:T(8,128)S(1)} %pad_maximum_fusion), channel_id=1, source_target_pairs={{0,224},{32,0},{64,32},{96,64},{128,96},{160,128},{192,160},{224,1... | collective-permute-start | bytes 196616 | tf_op jit(solution)/shard_map/ppermute | solution.py:292
  195.5 14.1 %all_to_all.25 = f32[16,16,256]{2,1,0:T(8,128)S(1)} all-to-all(f32[16,16,256]{2,1,0:T(8,128)S(1)} %bitcast.18), channel_id=1, replica_groups=mesh['z'=8,'xh'=2,'y'=4,'xl'=2,'core'=2] {'xh','y','xl'}, dimensions={0} | all-to-all | bytes 524288 | tf_op jit(solution)/shard_map/all_to_all | solution.py:360
  (51 shorter events, 29.5 us)
Async XLA Ops:
  3.2 24.2 %copy-start.3 = (s32[256]{0:T(256)S(1)}, s32[256]{0:T(256)}, u32[]{:S(2)}) copy-start(s32[256]{0:T(256)} %cell_ref.1) | copy-start | bytes 3076
  4.8 22.6 %all-to-all-start = ((f32[16,17,8,128]{3,2,1,0:T(8,128)}), f32[16,17,8,128]{3,2,1,0:T(8,128)S(1)}, u32[]{:S(2)}, u32[]{:S(2)}) async-start(f32[16,17,8,128]{3,2,1,0:T(8,128)} %get-tuple-element.12), calls=%async_computation | async-start | bytes 2228224 | tf_op jit(solution)/shard_map/all_to_all | solution.py:314
  34.1 31.7 %copy-start.4 = (s32[256]{0:T(256)S(1)}, s32[256]{0:T(256)}, u32[]{:S(2)}) copy-start(s32[256]{0:T(256)} %test_ref.1) | copy-start | bytes 3076
  34.1 31.7 %all-to-all-start.1 = ((f32[16,16,2,8,128]{4,3,2,1,0:T(8,128)}), f32[16,16,2,8,128]{4,3,2,1,0:T(8,128)S(1)}, u32[]{:S(2)}, u32[]{:S(2)}) async-start(f32[16,16,2,8,128]{4,3,2,1,0:T(8,128)} %shard_map.78), calls=%async_computation.1 | async-start | bytes 4194304 | tf_op jit(solution)/shard_map/all_to_all | solution.py:321
  37.9 3.5 %collective-permute-start = (f32[64,8,128]{2,1,0:T(8,128)S(1)}, f32[64,8,128]{2,1,0:T(8,128)S(1)}, u32[]{:S(2)}, u32[]{:S(2)}) collective-permute-start(f32[64,8,128]{2,1,0:T(8,128)S(1)} %bitcast.19), channel_id=1, source_target_pairs={{0,1},{1,2},{2,3},{3,4},{4,5},{5,6},{6,7},{7,8},{8,9},{9,10},{10,1... | collective-permute-start | bytes 786440 | tf_op jit(solution)/shard_map/ppermute | solution.py:306
  40.1 4.6 %collective-permute-start.1 = (f32[64,8,128]{2,1,0:T(8,128)S(1)}, f32[64,8,128]{2,1,0:T(8,128)S(1)}, u32[]{:S(2)}, u32[]{:S(2)}) collective-permute-start(f32[64,8,128]{2,1,0:T(8,128)S(1)} %bitcast.20), channel_id=1, source_target_pairs={{1,0},{2,1},{3,2},{4,3},{5,4},{6,5},{7,6},{8,7},{9,8},{10,9},{11,1... | collective-permute-start | bytes 786440 | tf_op jit(solution)/shard_map/ppermute | solution.py:307
  71.7 12.9 %collective-permute-start.2 = (f32[256,512]{1,0:T(8,128)S(1)}, f32[256,512]{1,0:T(8,128)S(1)}, u32[]{:S(2)}, u32[]{:S(2)}) collective-permute-start(f32[256,512]{1,0:T(8,128)S(1)} %get-tuple-element.15), channel_id=1, source_target_pairs={{0,16},{16,0},{1,17},{17,1},{2,18},{18,2},{3,19},{19,3},{4,20},{20... | collective-permute-start | bytes 1572872 | tf_op jit(solution)/shard_map/ppermute | solution.py:288
  72.5 18.0 %collective-permute-start.5 = (f32[256,512]{1,0:T(8,128)S(1)}, f32[256,512]{1,0:T(8,128)S(1)}, u32[]{:S(2)}, u32[]{:S(2)}) collective-permute-start(f32[256,512]{1,0:T(8,128)S(1)} %get-tuple-element.14.a0), channel_id=1, source_target_pairs={{0,32},{32,64},{64,96},{96,128},{128,160},{160,192},{192,224},{224... | collective-permute-start | bytes 1572872 | tf_op jit(solution)/shard_map/ppermute | solution.py:292
  74.5 16.1 %collective-permute-start.3 = (f32[256,512]{1,0:T(8,128)S(1)}, f32[256,512]{1,0:T(8,128)S(1)}, u32[]{:S(2)}, u32[]{:S(2)}) collective-permute-start(f32[256,512]{1,0:T(8,128)S(1)} %get-tuple-element.14.a0), channel_id=1, source_target_pairs={{0,224},{32,0},{64,32},{96,64},{128,96},{160,128},{192,160},{224,1... | collective-permute-start | bytes 1572872 | tf_op jit(solution)/shard_map/ppermute | solution.py:292
  84.7 15.9 %collective-permute-start.4 = (f32[256,512]{1,0:T(8,128)S(1)}, f32[256,512]{1,0:T(8,128)S(1)}, u32[]{:S(2)}, u32[]{:S(2)}) collective-permute-start(f32[256,512]{1,0:T(8,128)S(1)} %collective-permute-done.2.b0), channel_id=1, source_target_pairs={{0,224},{32,0},{64,32},{96,64},{128,96},{160,128},{192,160},{224,1... | collective-permute-start | bytes 1572872 | tf_op jit(solution)/shard_map/ppermute | solution.py:292
  90.5 14.0 %collective-permute-start.6 = (f32[256,512]{1,0:T(8,128)S(1)}, f32[256,512]{1,0:T(8,128)S(1)}, u32[]{:S(2)}, u32[]{:S(2)}) collective-permute-start(f32[256,512]{1,0:T(8,128)S(1)} %collective-permute-done.2.b0), channel_id=1, source_target_pairs={{0,32},{32,64},{64,96},{96,128},{128,160},{160,192},{192,224},{224... | collective-permute-start | bytes 1572872 | tf_op jit(solution)/shard_map/ppermute | solution.py:292
  90.5 25.2 %collective-permute-start.11 = (f32[256,512]{1,0:T(8,128)S(1)}, f32[256,512]{1,0:T(8,128)S(1)}, u32[]{:S(2)}, u32[]{:S(2)}) collective-permute-start(f32[256,512]{1,0:T(8,128)S(1)} %collective-permute-done.5.am), channel_id=1, source_target_pairs={{0,32},{32,64},{64,96},{96,128},{128,160},{160,192},{192,224},{224... | collective-permute-start | bytes 1572872 | tf_op jit(solution)/shard_map/ppermute | solution.py:292
  90.5 25.2 %collective-permute-start.9 = (f32[256,512]{1,0:T(8,128)S(1)}, f32[256,512]{1,0:T(8,128)S(1)}, u32[]{:S(2)}, u32[]{:S(2)}) collective-permute-start(f32[256,512]{1,0:T(8,128)S(1)} %collective-permute-done.3.a1), channel_id=1, source_target_pairs={{0,224},{32,0},{64,32},{96,64},{128,96},{160,128},{192,160},{224,1... | collective-permute-start | bytes 1572872 | tf_op jit(solution)/shard_map/ppermute | solution.py:292
  100.5 22.5 %collective-permute-start.10 = (f32[256,512]{1,0:T(8,128)S(1)}, f32[256,512]{1,0:T(8,128)S(1)}, u32[]{:S(2)}, u32[]{:S(2)}) collective-permute-start(f32[256,512]{1,0:T(8,128)S(1)} %collective-permute-done.4.b1), channel_id=1, source_target_pairs={{0,224},{32,0},{64,32},{96,64},{128,96},{160,128},{192,160},{224,1... | collective-permute-start | bytes 1572872 | tf_op jit(solution)/shard_map/ppermute | solution.py:292
  104.5 22.5 %collective-permute-start.12 = (f32[256,512]{1,0:T(8,128)S(1)}, f32[256,512]{1,0:T(8,128)S(1)}, u32[]{:S(2)}, u32[]{:S(2)}) collective-permute-start(f32[256,512]{1,0:T(8,128)S(1)} %collective-permute-done.6.bm), channel_id=1, source_target_pairs={{0,32},{32,64},{64,96},{96,128},{128,160},{160,192},{192,224},{224... | collective-permute-start | bytes 1572872 | tf_op jit(solution)/shard_map/ppermute | solution.py:292
  109.5 38.0 %collective-permute-start.7 = (f32[16,6,16,256]{3,2,1,0:T(8,128)}, f32[16,6,16,256]{3,2,1,0:T(8,128)}, u32[]{:S(2)}, u32[]{:S(2)}) collective-permute-start(f32[16,6,16,256]{3,2,1,0:T(8,128)} %get-tuple-element.17), channel_id=1, source_target_pairs={{0,1},{1,0},{2,3},{3,2},{4,5},{5,4},{6,7},{7,6},{8,9},{9,8},{10,11... | collective-permute-start | bytes 4718600 | tf_op jit(solution)/shard_map/ppermute | solution.py:288
  129.6 3.8 %collective-permute-start.13 = (f32[16,3,16,256]{3,2,1,0:T(8,128)S(1)}, f32[16,3,16,256]{3,2,1,0:T(8,128)S(1)}, u32[]{:S(2)}, u32[]{:S(2)}) collective-permute-start(f32[16,3,16,256]{3,2,1,0:T(8,128)S(1)} %get-tuple-element.19), channel_id=1, source_target_pairs={{0,1},{1,0},{2,3},{3,2},{4,5},{5,4},{6,7},{7,6},{8,9},{9,8},{10,11... | collective-permute-start | bytes 2359304 | tf_op jit(solution)/shard_map/ppermute | solution.py:288
  134.5 25.1 %all-to-all-start.3 = ((f32[16,3,16,256]{3,2,1,0:T(8,128)}), f32[16,3,16,256]{3,2,1,0:T(8,128)S(1)}, u32[]{:S(2)}, u32[]{:S(2)}) async-start(f32[16,3,16,256]{3,2,1,0:T(8,128)} %add.28), calls=%async_computation.3 | async-start | bytes 1572864 | tf_op jit(solution)/shard_map/all_to_all | solution.py:345
  159.6 27.8 %all-to-all-start.2 = ((f32[16,6,16,256]{3,2,1,0:T(8,128)}), f32[16,6,16,256]{3,2,1,0:T(8,128)S(1)}, u32[]{:S(2)}, u32[]{:S(2)}) async-start(f32[16,6,16,256]{3,2,1,0:T(8,128)} %add.27), calls=%async_computation.2 | async-start | bytes 3145728 | tf_op jit(solution)/shard_map/all_to_all | solution.py:345
  166.3 24.5 %collective-permute-start.15 = (f32[3,16,256]{2,1,0:T(8,128)S(1)}, f32[3,16,256]{2,1,0:T(8,128)S(1)}, u32[]{:S(2)}, u32[]{:S(2)}) collective-permute-start(f32[3,16,256]{2,1,0:T(8,128)S(1)} %shard_map.83), channel_id=1, source_target_pairs={{0,64},{32,96},{64,128},{96,160},{128,192},{160,224},{192,0},{224,... | collective-permute-start | bytes 147464 | tf_op jit(solution)/shard_map/ppermute | solution.py:292
  166.5 24.4 %collective-permute-start.16 = (f32[1,16,256]{2,1,0:T(8,128)S(1)}, f32[1,16,256]{2,1,0:T(8,128)S(1)}, u32[]{:S(2)}, u32[]{:S(2)}) collective-permute-start(f32[1,16,256]{2,1,0:T(8,128)S(1)} %slice.19), channel_id=1, source_target_pairs={{0,192},{32,224},{64,0},{96,32},{128,64},{160,96},{192,128},{224,1... | collective-permute-start | bytes 49160 | tf_op jit(solution)/shard_map/ppermute | solution.py:292
  187.5 5.6 %collective-permute-start.8 = (f32[4,16,256]{2,1,0:T(8,128)S(1)}, f32[4,16,256]{2,1,0:T(8,128)S(1)}, u32[]{:S(2)}, u32[]{:S(2)}) collective-permute-start(f32[4,16,256]{2,1,0:T(8,128)S(1)} %slice.16), channel_id=1, source_target_pairs={{0,32},{32,64},{64,96},{96,128},{128,160},{160,192},{192,224},{224... | collective-permute-start | bytes 196616 | tf_op jit(solution)/shard_map/ppermute | solution.py:292
  187.6 6.1 %collective-permute-start.14 = (f32[4,16,256]{2,1,0:T(8,128)S(1)}, f32[4,16,256]{2,1,0:T(8,128)S(1)}, u32[]{:S(2)}, u32[]{:S(2)}) collective-permute-start(f32[4,16,256]{2,1,0:T(8,128)S(1)} %pad_maximum_fusion), channel_id=1, source_target_pairs={{0,224},{32,0},{64,32},{96,64},{128,96},{160,128},{192,160},{224,1... | collective-permute-start | bytes 196616 | tf_op jit(solution)/shard_map/ppermute | solution.py:292
  193.6 1.3 collective-permute-start.17
  (4 other events, 6.4 us)

commit v2 on v1

v2 whole, which is shorter than its diff:
```python
import functools

import jax
import jax.numpy as jnp
from jax import lax
from jax.experimental import pallas as pl
from jax.experimental.pallas import tpu as pltpu
from jax.sharding import PartitionSpec as P

SWEEPS = 3
SOURCE = 16.0
CENTRE = 1.075
HALFWIDTH = 0.925

OBS_AXES = ("z", "xh")
CELL_AXES = ("y", "xl", "core")
PLANE = ("xh", "y", "xl")
LAYERS = 16
GROUP = 16
ROWS = 256
TESTS = 64
NY, NZ = 8, 128
F32, BF16 = jnp.float32, jnp.bfloat16

VMEM = pl.BlockSpec(memory_space=pltpu.VMEM)
SMEM = pl.BlockSpec(memory_space=pltpu.SMEM)
HBM = pl.BlockSpec(memory_space=pltpu.HBM)


def call(kernel, outs, specs, scratch=(), flops=0, moved=0):
    return pl.pallas_call(
        kernel,
        out_shape=outs,
        in_specs=specs,
        out_specs=jax.tree.map(lambda _: VMEM, outs),
        scratch_shapes=list(scratch),
        compiler_params=pltpu.CompilerParams(vmem_limit_bytes=40 * 2**20),
        cost_estimate=pl.CostEstimate(flops=flops, bytes_accessed=moved, transcendentals=0),
    )


def shape(*dims, dtype=F32):
    return jax.ShapeDtypeStruct(dims, dtype)


def places():
    row = lax.broadcasted_iota(jnp.int32, (NY, NZ), 0)
    col = lax.broadcasted_iota(jnp.int32, (NY, NZ), 1)
    return row, col


def beside(v):
    return (
        pltpu.roll(v, 1, 0),
        pltpu.roll(v, NY - 1, 0),
        pltpu.roll(v, 1, 1),
        pltpu.roll(v, NZ - 1, 1),
    )


def inside():
    row, col = places()
    return (row > 0, row < NY - 1, col > 0, col < NZ - 1)


def pack_kernel(
    logk_hbm, test_hbm, label_hbm, start_hbm, heads_hbm, packed_hbm,
    logk_ref, test_ref, label_ref, heads_ref, packed_ref, sems,
):
    moves = [
        pltpu.make_async_copy(source, target, sems.at[i])
        for i, (source, target) in enumerate((
            (heads_hbm, heads_ref),
            (test_hbm, test_ref),
            (logk_hbm, logk_ref),
            (label_hbm, label_ref),
            (start_hbm, packed_ref.at[:, pl.ds(0, GROUP)]),
        ))
    ]
    for move in moves:
        move.start()
    moves[2].wait()
    moves[3].wait()
    label = label_ref[0]
    logk = jnp.zeros((NY, NZ), F32)
    for zone in range(logk_ref.shape[0]):
        logk = jnp.where(label == zone, logk_ref[zone], logk)
    conduct = jnp.exp(logk)
    moves[0].wait()
    moves[1].wait()

    def one(target, carry):
        for k in range(GROUP):
            packed_ref[target, GROUP + k] = heads_ref[test_ref[target * GROUP + k]]
        packed_ref[target, 2 * GROUP] = conduct
        return carry

    lax.fori_loop(0, LAYERS, one, 0)
    moves[4].wait()
    out = pltpu.make_async_copy(packed_ref, packed_hbm, sems.at[5])
    out.start()
    out.wait()


def sweep_kernel(me_ref, cell_ref, got_ref, panel_ref, out_ref, weight_ref, source_ref):
    row, col = places()
    flat = row * NZ + col
    inner = inside()
    mask = [jnp.where(ok, 1.0, 0.0).astype(F32) for ok in inner]

    def along_x(v, layer):
        if layer == 0:
            return v[1]
        if layer + 1 == LAYERS:
            return -v[layer - 1]
        return v[layer + 1] - v[layer - 1]

    def along_y(v):
        return mask[1] * pltpu.roll(v, NY - 1, 0) - mask[0] * pltpu.roll(v, 1, 0)

    def along_z(v):
        return mask[3] * pltpu.roll(v, NZ - 1, 1) - mask[2] * pltpu.roll(v, 1, 1)

    def face(a, b):
        return 2.0 * a * b / (a + b)

    below = None
    for layer in range(LAYERS):
        here = got_ref[layer, 2 * GROUP]
        above = face(here, got_ref[layer + 1, 2 * GROUP]) if layer + 1 < LAYERS else None
        edge = [face(here, b) for b in beside(here)]
        faces = [here if below is None else below, here if above is None else above]
        faces += [jnp.where(ok, w, here) for ok, w in zip(inner, edge)]
        diagonal = faces[0]
        for extra in faces[1:]:
            diagonal = diagonal + extra
        inverse = 1.0 / diagonal
        if below is not None:
            weight_ref[layer, 0] = below * inverse
        if above is not None:
            weight_ref[layer, 1] = above * inverse
        for i, (ok, w) in enumerate(zip(inner, edge)):
            weight_ref[layer, 2 + i] = jnp.where(ok, w, 0.0) * inverse
        weight_ref[layer, 6] = inverse
        source_ref[layer] = jnp.zeros((NY, NZ), F32)
        below = above

    ratio = CENTRE / HALFWIDTH
    first = me_ref[0] * GROUP

    def one(k, carry):
        cell = cell_ref[first + k]
        layer_of = cell // (NY * NZ)
        hit = flat == cell - layer_of * (NY * NZ)
        source_ref[layer_of] = jnp.where(hit, SOURCE * weight_ref[layer_of, 6], 0.0)
        v = [got_ref[layer, k] for layer in range(LAYERS)]
        update = None
        damping = 1.0 / ratio
        for sweep in range(SWEEPS):
            misfit = []
            for layer in range(LAYERS):
                m = source_ref[layer] - v[layer]
                if layer > 0:
                    m = m + weight_ref[layer, 0] * v[layer - 1]
                if layer + 1 < LAYERS:
                    m = m + weight_ref[layer, 1] * v[layer + 1]
                for i, b in enumerate(beside(v[layer])):
                    m = m + weight_ref[layer, 2 + i] * b
                misfit.append(m)
            if sweep == 0:
                update = [m * (1.0 / CENTRE) for m in misfit]
            else:
                newer = 1.0 / (2.0 * ratio - damping)
                keep, add = newer * damping, 2.0 * newer / HALFWIDTH
                update = [keep * u + add * m for u, m in zip(update, misfit)]
                damping = newer
            v = [a + u for a, u in zip(v, update)]
        h = [got_ref[layer, GROUP + k] for layer in range(LAYERS)]
        for layer in range(LAYERS):
            total = along_x(v, layer) * along_x(h, layer)
            total = total + along_y(v[layer]) * along_y(h[layer])
            total = total + along_z(v[layer]) * along_z(h[layer])
            here = pl.ds(pl.multiple_of(k * NY, NY), NY)
            out_ref[layer, here, :] = (-0.25 * got_ref[layer, 2 * GROUP]) * total
        source_ref[layer_of] = jnp.zeros((NY, NZ), F32)
        return carry

    lax.fori_loop(0, GROUP, one, 0)

    def panel(layer, carry):
        for part in range(2):
            for i in range(NY // 2):
                at = part * (NY // 2) + i
                rows = out_ref[layer, pl.ds(at, GROUP, stride=NY), :]
                panel_ref[part * LAYERS + layer, :, pl.ds(i * NZ, NZ)] = rows
        return carry

    lax.fori_loop(0, LAYERS, panel, 0)


def split_into(ref, high_ref, low_ref, at):
    x = ref[...]
    high = x.astype(BF16)
    high_ref[at] = high
    low_ref[at] = (x - high.astype(F32)).astype(BF16)


def product(high_ref, low_ref, left, right):
    def dot(a, b):
        return lax.dot_general(a, b, (((1,), (1,)), ((), ())), preferred_element_type=F32)

    lh, ll = high_ref[left], low_ref[left]
    rh, rl = high_ref[right], low_ref[right]
    return dot(lh, rh) + (dot(lh, rl) + dot(ll, rh))


def rows_of(which):
    return pl.ds(pl.multiple_of(which * ROWS, ROWS), ROWS)


def pair_kernel(pairs, me_ref, *refs):
    blocks, (mine_ref, theirs_ref, high_ref, low_ref) = refs[:-4], refs[-4:]
    for at, ref in enumerate(blocks):
        split_into(ref, high_ref, low_ref, at)
    core = me_ref[2]
    for side, out_ref in enumerate((mine_ref, theirs_ref)):
        right = rows_of(side ^ core)
        for i, (a, b) in enumerate(pairs):
            for half in range(2):
                block = product(high_ref, low_ref, (a, rows_of(half)), (b, right))
                out_ref[half, :, i] = block.reshape(8, 32, ROWS)


def sens_kernel(me_ref, panel_ref, got_ref, sens_ref):
    xh = me_ref[1]

    def eight(block, carry):
        own = pl.ds(pl.multiple_of(xh * ROWS + block * 8, 8), 8)
        here = pl.ds(pl.multiple_of(block * 8, 8), 8)
        at = block * (8 * NY)
        for i in range(NY // 2):
            lanes = pl.ds(i * NZ, NZ)
            sens_ref[pl.ds(at + xh * (NY // 2) + i, 8, stride=NY), :] = panel_ref[own, lanes]
            sens_ref[pl.ds(at + (1 - xh) * (NY // 2) + i, 8, stride=NY), :] = got_ref[here, lanes]
        return carry

    lax.fori_loop(0, ROWS // 8, eight, 0, unroll=4)


def total_kernel(parts_ref, out_ref):
    total = parts_ref[0]
    for i in range(1, parts_ref.shape[0]):
        total = total + parts_ref[i]
    out_ref[...] = total


def place_kernel(me_ref, d0, d12, up1, down1, far_down1, up2, down2, slot_ref):
    z = me_ref[3]
    sources = (d0[0], d12[0], down1[0], far_down1[0], down2[0], up2[0], up1[1], up1[0])
    for r, source in enumerate(sources):
        slot_ref[(z + r) % 8] = source


def finish_kernel(me_ref, block_ref, out_ref):
    flip = me_ref[4] == 1
    scale = 1.0 / (LAYERS * NY * NZ)

    @pl.when(flip)
    def _():
        out_ref[...] = block_ref[...].T * scale

    @pl.when(jnp.logical_not(flip))
    def _():
        out_ref[...] = block_ref[...] * scale


def swap(x, axis):
    return lax.ppermute(x, axis, [(0, 1), (1, 0)])


def round_z(x, by):
    return lax.ppermute(x, "z", [(i, (i + by) % 8) for i in range(8)])


def turn_z(x, by):
    pairs = [
        ((z * 2 + a) * 2 + b, (((z + by) % 8) * 2 + b) * 2 + a)
        for z in range(8) for a in range(2) for b in range(2)
    ]
    return lax.ppermute(x, ("z", "xh", "core"), pairs)


def per_device(adjoint_start, forward_heads, zone_label, zone_logk, obs_cell, test_of_obs):
    cells = lax.axis_index(CELL_AXES)
    xh, core, z = lax.axis_index("xh"), lax.axis_index("core"), lax.axis_index("z")
    z2 = lax.axis_index(("y", "xl"))
    flip = ((z2 - z + 8) % 8 >= 5).astype(jnp.int32)
    me = jnp.stack([cells, xh, core, z, flip, flip, flip, flip]).astype(jnp.int32)

    packed = pl.pallas_call(
        pack_kernel,
        out_shape=shape(LAYERS, 2 * GROUP + 1, NY, NZ),
        in_specs=[HBM] * 5,
        out_specs=HBM,
        scratch_shapes=[
            pltpu.SMEM((zone_logk.shape[0],), F32),
            pltpu.SMEM((ROWS,), jnp.int32),
            pltpu.VMEM((1, NY, NZ), jnp.int32),
            pltpu.VMEM((TESTS, NY, NZ), F32),
            pltpu.VMEM((LAYERS, 2 * GROUP + 1, NY, NZ), F32),
            pltpu.SemaphoreType.DMA((6,)),
        ],
        compiler_params=pltpu.CompilerParams(vmem_limit_bytes=60 * 2**20),
    )(
        zone_logk, test_of_obs, zone_label,
        adjoint_start.reshape(LAYERS, GROUP, NY, NZ), forward_heads.reshape(TESTS, NY, NZ),
    )
    got = lax.all_to_all(packed, CELL_AXES, 0, 0, tiled=True)
    half = NY * NZ // 2
    panel = call(
        sweep_kernel,
        shape(2 * LAYERS, GROUP, half),
        [SMEM, SMEM, VMEM],
        [
            pltpu.VMEM((LAYERS, GROUP * NY, NZ), F32),
            pltpu.VMEM((LAYERS, 7, NY, NZ), F32),
            pltpu.VMEM((LAYERS, NY, NZ), F32),
        ],
    )(me, obs_cell, got)
    x0 = lax.all_to_all(panel, ("xh",) + CELL_AXES, 0, 0, tiled=True).reshape(2 * ROWS, half)
    x1, xm = round_z(x0, -1), round_z(x0, 1)
    other = swap(lax.dynamic_slice(x0, ((1 - xh) * ROWS, 0), (ROWS, half)), "xh")
    x2, xn = round_z(x1, -1), round_z(xm, 1)

    def partial(pairs, *blocks):
        count = len(pairs)
        out = shape(2, 8, count, 32, ROWS)
        mine, theirs = call(
            functools.partial(pair_kernel, pairs),
            (out, out),
            [SMEM] + [VMEM] * len(blocks),
            [pltpu.VMEM((len(blocks), 2 * ROWS, half), BF16)] * 2,
            flops=24 * count * ROWS * ROWS * half, moved=2**23,
        )(me, *blocks)
        return mine + swap(theirs, "core")

    def exchange(parts):
        parts = parts.reshape(16, parts.shape[2], 32, ROWS)
        return lax.all_to_all(parts, PLANE, 0, 0, tiled=True)

    def total(parts):
        return call(total_kernel, shape(*parts.shape[1:]), [VMEM])(parts)

    d0 = exchange(partial(((0, 0),), x0))
    x1, xm, d0, other = lax.optimization_barrier((x1, xm, d0, other))
    d12 = partial(((0, 1), (2, 1)), x0, x1, xm)
    d12, other = lax.optimization_barrier((d12, other))
    sens = call(sens_kernel, shape(ROWS * NY, NZ), [SMEM, VMEM, VMEM])(me, x0, other)
    d12 = exchange(d12)
    d12, x2, xn, sens = lax.optimization_barrier((d12, x2, xn, sens))
    far = total(exchange(partial(((0, 1), (2, 1)), xm, x2, xn)))
    d0, d12 = total(d0), total(d12)

    slots = call(place_kernel, shape(8, 32, ROWS), [SMEM] + [VMEM] * 7)(
        me, d0, d12,
        turn_z(d12, 1), round_z(d12[1:2], -1),
        round_z(far[0:1], -1), turn_z(far[0:1], 2), round_z(far[1:2], -2),
    )
    block = lax.all_to_all(slots, ("y", "xl"), 0, 0, tiled=True)
    gram = call(finish_kernel, shape(ROWS, ROWS), [SMEM, VMEM])(me, block.reshape(ROWS, ROWS))
    return sens.reshape(ROWS, 1, NY, NZ), gram


def solution(mesh):
    fine = jax.sharding.Mesh(
        mesh.devices.reshape(8, 2, 4, 2, 2), ("z", "xh", "y", "xl", "core")
    )
    return jax.shard_map(
        per_device,
        mesh=fine,
        in_specs=(
            P(OBS_AXES, CELL_AXES, None, None),
            P(None, CELL_AXES, None, None),
            P(CELL_AXES, None, None),
            P(),
            P(OBS_AXES),
            P(OBS_AXES),
        ),
        out_specs=(P(OBS_AXES, CELL_AXES, None, None), P(OBS_AXES, CELL_AXES)),
        check_vma=False,
    )
```

time: 213 us -> 184 us (0.86)
  starting transfers between devices: 65.5 us -> 42.9 us
  waiting for transfers between devices: 99.5 us -> 79.3 us
  blocking collectives: 14.1 us -> 32.7 us
    all_to_all x3, waiting for transfers between devices: 47 us -> 19.6 us  [exchange(): return lax.all_to_all(parts, PLANE, 0, 0, tiled=True)]
    all_to_all x1 -> x2, blocking collectives: 14.1 us -> 32.7 us  [the longest x1 20.6 us: per_device(): lax.all_to_all(panel, ('xh',) + CELL_AXES, 0, 0, tiled=True)]
    all_to_all x1, waiting for transfers between devices: 17.2 us -> 28.5 us  [per_device(): got = lax.all_to_all(packed, CELL_AXES, 0, 0, tiled=True)]
    ppermute x12 -> x7, starting transfers between devices: 26.2 us -> 15.1 us  [round_z(): return lax.ppermute(x, 'z', [(i, (i + by) % 8) for i in range(8)])]
    ppermute x12 -> x7, waiting for transfers between devices: 22.5 us -> 17.7 us  [round_z(): return lax.ppermute(x, 'z', [(i, (i + by) % 8) for i in range(8)])]
    ppermute x4, starting transfers between devices: 6.97 us -> 2.52 us  [swap(): return lax.ppermute(x, axis, [(0, 1), (1, 0)])]
    all_to_all x3, starting transfers between devices: 23.6 us -> 19.6 us  [exchange(): return lax.all_to_all(parts, PLANE, 0, 0, tiled=True)]
    ppermute x2, starting transfers between devices: 3.5 us -> 0.43 us  [turn_z(): return lax.ppermute(x, ('z', 'xh', 'core'), pairs)]
  transfers between devices with their start and end apart: 22 -> 17, of which waited for: 14 -> 9; matrix products, arithmetic and copies ran while one was open for 2% -> 2% of each run, Pallas kernels for 4% -> 2%
where the time goes in v2:
time: 184 us; the launch traced here: 183 us
  waiting for transfers between devices  79.3 us (43%)
  starting transfers between devices  42.9 us (23%)
  blocking collectives  32.7 us (18%)
  Pallas kernels  23.2 us (13%)
  other arithmetic  3.22 us (2%)
    all_to_all x1, waiting for transfers between devices, per_device(): got = lax.all_to_all(packed, CELL_AXES, 0, 0, tiled=True)  28.5 us
    all_to_all x1, blocking collectives, per_device(): lax.all_to_all(panel, ('xh',) + CELL_AXES, 0, 0, tiled=True)  20.6 us
    all_to_all x3, starting transfers between devices, exchange(): return lax.all_to_all(parts, PLANE, 0, 0, tiled=True)  19.6 us
    all_to_all x3, waiting for transfers between devices, exchange(): return lax.all_to_all(parts, PLANE, 0, 0, tiled=True)  19.6 us
    ppermute x7, waiting for transfers between devices, round_z(): return lax.ppermute(x, 'z', [(i, (i + by) % 8) for i in range(8)])  17.7 us
    ppermute x7, starting transfers between devices, round_z(): return lax.ppermute(x, 'z', [(i, (i + by) % 8) for i in range(8)])  15.1 us
    all_to_all x1, blocking collectives, per_device(): block = lax.all_to_all(slots, ('y', 'xl'), 0, 0, tiled=True)  12.1 us
    pallas_call x3, Pallas kernels, partial(): call(functools.partial(pair_kernel, pairs), (out, out), [SMEM] + [VMEM] *...  10.1 us
  transfers between devices with their start and end apart: 17, of which 9 were waited for; matrix products, arithmetic and copies ran while one was open for 2% of the time, Pallas kernels for 2%

profile of v2, /device:TPU:4, one launch (start us, length us, event | category | flops | bytes accessed | tf_op | source)
XLA Modules:
  0.0 183.1 jit_solution(2891397455823181705)
XLA Ops:
  0.6 2.7 %shard_map.77 = f32[16,33,8,128]{3,2,1,0:T(8,128)} custom-call(f32[16]{0:T(128)} %logk_hbm.1, s32[256]{0:T(256)} %test_hbm.1, s32[1,8,128]{2,1,0:T(8,128)} %label_hbm.1, f32[16,16,8,128]{3,2,1,0:T(8,128)} %bitcast.24, f32[64,8,128]{2,1,0:T(8,128)} %bitcast.26), custom_call_target="tpu_custom_call" | custom-call | tf_op jit(solution)/shard_map/pallas_call | solution.py:300
  3.4 5.2 %all-to-all-start = ((f32[16,33,8,128]{3,2,1,0:T(8,128)}), f32[16,33,8,128]{3,2,1,0:T(8,128)S(1)}, u32[]{:S(2)}, u32[]{:S(2)}) async-start(f32[16,33,8,128]{3,2,1,0:T(8,128)} %shard_map.77), calls=%async_computation | async-start | bytes 4325376 | tf_op jit(solution)/shard_map/all_to_all | solution.py:318
  8.7 28.5 %all-to-all-done.got_ref = f32[16,33,8,128]{3,2,1,0:T(8,128)S(1)} async-done(((f32[16,33,8,128]{3,2,1,0:T(8,128)}), f32[16,33,8,128]{3,2,1,0:T(8,128)S(1)}, u32[]{:S(2)}, u32[]{:S(2)}) %all-to-all-start) | async-done | bytes 2162720 | tf_op jit(solution)/shard_map/all_to_all | solution.py:318
  37.2 6.6 %shard_map.78 = f32[32,16,512]{2,1,0:T(8,128)S(1)} custom-call(s32[8]{0:T(128)S(1)} %stack.30.me_ref, s32[256]{0:T(256)S(1)} %copy-done, f32[16,33,8,128]{3,2,1,0:T(8,128)S(1)} %all-to-all-done.got_ref), custom_call_target="tpu_custom_call" | custom-call | tf_op jit(solution)/shard_map/pallas_call | solution.py:320
  43.8 20.6 %all_to_all.30 = f32[32,16,512]{2,1,0:T(8,128)S(1)} all-to-all(f32[32,16,512]{2,1,0:T(8,128)S(1)} %shard_map.78), channel_id=1, replica_groups=mesh['z'=8,'xh'=2,'y'=4,'xl'=2,'core'=2] {'xh','y','xl','core'}, dimensions={0} | all-to-all | bytes 2097152 | tf_op jit(solution)/shard_map/all_to_all | solution.py:330
  64.4 5.9 %collective-permute-start = (f32[512,512]{1,0:T(8,128)S(1)}, f32[512,512]{1,0:T(8,128)}, u32[]{:S(2)}, u32[]{:S(2)}) collective-permute-start(f32[512,512]{1,0:T(8,128)S(1)} %bitcast.15), channel_id=1, source_target_pairs={{0,224},{32,0},{64,32},{96,64},{128,96},{160,128},{192,160},{224,1... | collective-permute-start | bytes 3145736 | tf_op jit(solution)/shard_map/ppermute | solution.py:282
  72.9 2.2 %collective-permute-start.3 = (f32[256,512]{1,0:T(8,128)}, f32[256,512]{1,0:T(8,128)S(1)}, u32[]{:S(2)}, u32[]{:S(2)}) collective-permute-start(f32[256,512]{1,0:T(8,128)} %constant_dynamic-slice_fusion), channel_id=1, source_target_pairs={{0,16},{16,0},{1,17},{17,1},{2,18},{18,2},{3,19},{19,3},{4,20},{20... | collective-permute-start | bytes 1572872 | tf_op jit(solution)/shard_map/ppermute | solution.py:278
  76.0 6.0 %all-to-all-start.2 = ((f32[16,1,32,256]{3,2,1,0:T(8,128)}), f32[16,1,32,256]{3,2,1,0:T(8,128)S(1)}, u32[]{:S(2)}, u32[]{:S(2)}) async-start(f32[16,1,32,256]{3,2,1,0:T(8,128)} %bitcast.8), calls=%async_computation.2 | async-start | bytes 1048576 | tf_op jit(solution)/shard_map/all_to_all | solution.py:349
  82.0 7.4 %collective-permute-done.3.got_ref = f32[256,512]{1,0:T(8,128)S(1)} collective-permute-done((f32[256,512]{1,0:T(8,128)}, f32[256,512]{1,0:T(8,128)S(1)}, u32[]{:S(2)}, u32[]{:S(2)}) %collective-permute-start.3) | collective-permute-done | bytes 524320 | tf_op jit(solution)/shard_map/ppermute | solution.py:278
  89.4 6.3 %all-to-all-done.2.parts_ref = f32[16,1,32,256]{3,2,1,0:T(8,128)S(1)} async-done(((f32[16,1,32,256]{3,2,1,0:T(8,128)}), f32[16,1,32,256]{3,2,1,0:T(8,128)S(1)}, u32[]{:S(2)}, u32[]{:S(2)}) %all-to-all-start.2) | async-done | bytes 524320 | tf_op jit(solution)/shard_map/all_to_all | solution.py:349
  96.4 4.1 %shard_map.80 = (f32[2,8,2,32,256]{4,3,2,1,0:T(8,128)S(1)}, f32[2,8,2,32,256]{4,3,2,1,0:T(8,128)S(1)}) custom-call(s32[8]{0:T(128)S(1)} %stack.30.me_ref, f32[512,512]{1,0:T(8,128)S(1)} %bitcast.19, f32[512,512]{1,0:T(8,128)} %collective-permute-done.refs_1_, f32[512,512]{1,0:T(8,128)} %collective-permute-done.1.refs_2_.refs_0_), custom_call_target="tpu_custom_call" | custom-call | flops 1610612736 | bytes 8388608 | tf_op jit(solution)/shard_map/pallas_call | solution.py:338
  100.6 2.6 %collective-permute-start.5 = (f32[512,512]{1,0:T(8,128)}, f32[512,512]{1,0:T(8,128)}, u32[]{:S(2)}, u32[]{:S(2)}) collective-permute-start(f32[512,512]{1,0:T(8,128)} %collective-permute-done.refs_1_), channel_id=1, source_target_pairs={{0,224},{32,0},{64,32},{96,64},{128,96},{160,128},{192,160},{224,1... | collective-permute-start | bytes 3145736 | tf_op jit(solution)/shard_map/ppermute | solution.py:282
  104.4 6.8 %all-to-all-start.3 = ((f32[16,2,32,256]{3,2,1,0:T(8,128)}), f32[16,2,32,256]{3,2,1,0:T(8,128)S(1)}, u32[]{:S(2)}, u32[]{:S(2)}) async-start(f32[16,2,32,256]{3,2,1,0:T(8,128)} %bitcast.23), calls=%async_computation.3 | async-start | bytes 2097152 | tf_op jit(solution)/shard_map/all_to_all | solution.py:349
  111.3 1.7 shard_map.81
  113.0 13.6 %collective-permute-done.5.refs_1_ = f32[512,512]{1,0:T(8,128)} collective-permute-done((f32[512,512]{1,0:T(8,128)}, f32[512,512]{1,0:T(8,128)}, u32[]{:S(2)}, u32[]{:S(2)}) %collective-permute-start.5) | collective-permute-done | bytes 1048608 | tf_op jit(solution)/shard_map/ppermute | solution.py:282
  126.6 3.4 %collective-permute-done.6.refs_2_ = f32[512,512]{1,0:T(8,128)} collective-permute-done((f32[512,512]{1,0:T(8,128)}, f32[512,512]{1,0:T(8,128)}, u32[]{:S(2)}, u32[]{:S(2)}) %collective-permute-start.6) | collective-permute-done | bytes 1048608 | tf_op jit(solution)/shard_map/ppermute | solution.py:282
  130.0 4.4 %shard_map.84 = (f32[2,8,2,32,256]{4,3,2,1,0:T(8,128)S(1)}, f32[2,8,2,32,256]{4,3,2,1,0:T(8,128)S(1)}) custom-call(s32[8]{0:T(128)S(1)} %stack.30.me_ref, f32[512,512]{1,0:T(8,128)} %collective-permute-done.1.refs_2_.refs_0_, f32[512,512]{1,0:T(8,128)} %collective-permute-done.5.refs_1_, f32[512,512]{1,0:T(8,128)} %collective-permute-done.6.refs_2_), custom_call_target="tpu_custom_call" | custom-call | flops 1610612736 | bytes 8388608 | tf_op jit(solution)/shard_map/pallas_call | solution.py:338
  134.5 2.6 %collective-permute-done.9 = f32[2,8,2,32,256]{4,3,2,1,0:T(8,128)S(1)} collective-permute-done((f32[2,8,2,32,256]{4,3,2,1,0:T(8,128)S(1)}, f32[2,8,2,32,256]{4,3,2,1,0:T(8,128)S(1)}, u32[]{:S(2)}, u32[]{:S(2)}) %collective-permute-start.9) | collective-permute-done | bytes 1048608 | tf_op jit(solution)/shard_map/ppermute | solution.py:278
  138.3 6.8 %all-to-all-start.4 = ((f32[16,2,32,256]{3,2,1,0:T(8,128)}), f32[16,2,32,256]{3,2,1,0:T(8,128)S(1)}, u32[]{:S(2)}, u32[]{:S(2)}) async-start(f32[16,2,32,256]{3,2,1,0:T(8,128)} %bitcast.22), calls=%async_computation.4 | async-start | bytes 2097152 | tf_op jit(solution)/shard_map/all_to_all | solution.py:349
  145.2 2.2 %collective-permute-start.8 = (f32[1,32,256]{2,1,0:T(8,128)S(1)}, f32[1,32,256]{2,1,0:T(8,128)S(1)}, u32[]{:S(2)}, u32[]{:S(2)}) collective-permute-start(f32[1,32,256]{2,1,0:T(8,128)S(1)} %slice.13), channel_id=1, source_target_pairs={{0,224},{32,0},{64,32},{96,64},{128,96},{160,128},{192,160},{224,1... | collective-permute-start | bytes 98312 | tf_op jit(solution)/shard_map/ppermute | solution.py:282
  147.5 13.3 %all-to-all-done.4.parts_ref = f32[16,2,32,256]{3,2,1,0:T(8,128)S(1)} async-done(((f32[16,2,32,256]{3,2,1,0:T(8,128)}), f32[16,2,32,256]{3,2,1,0:T(8,128)S(1)}, u32[]{:S(2)}, u32[]{:S(2)}) %all-to-all-start.4) | async-done | bytes 1048608 | tf_op jit(solution)/shard_map/all_to_all | solution.py:349
  161.5 4.0 %collective-permute-start.12 = (f32[1,32,256]{2,1,0:T(8,128)S(1)}, f32[1,32,256]{2,1,0:T(8,128)S(1)}, u32[]{:S(2)}, u32[]{:S(2)}) collective-permute-start(f32[1,32,256]{2,1,0:T(8,128)S(1)} %get-tuple-element.36), channel_id=1, source_target_pairs={{0,192},{32,224},{64,0},{96,32},{128,64},{160,96},{192,128},{224,1... | collective-permute-start | bytes 98312 | tf_op jit(solution)/shard_map/ppermute | solution.py:282
  165.6 3.5 %collective-permute-done.11.up2 = f32[1,32,256]{2,1,0:T(8,128)S(1)} collective-permute-done((f32[1,32,256]{2,1,0:T(8,128)S(1)}, f32[1,32,256]{2,1,0:T(8,128)S(1)}, u32[]{:S(2)}, u32[]{:S(2)}) %collective-permute-start.11) | collective-permute-done | bytes 32800 | tf_op jit(solution)/shard_map/ppermute | solution.py:290
  169.7 12.1 %all_to_all.31 = f32[8,32,256]{2,1,0:T(8,128)S(1)} all-to-all(f32[8,32,256]{2,1,0:T(8,128)S(1)} %shard_map.86), channel_id=1, replica_groups=mesh['z'=8,'xh'=2,'y'=4,'xl'=2,'core'=2] {'y','xl'}, dimensions={0} | all-to-all | bytes 524288 | tf_op jit(solution)/shard_map/all_to_all | solution.py:369
  (32 shorter events, 9.6 us)
Async XLA Ops:
  3.4 33.8 %copy-start = (s32[256]{0:T(256)S(1)}, s32[256]{0:T(256)}, u32[]{:S(2)}) copy-start(s32[256]{0:T(256)} %cell_ref.1) | copy-start | bytes 3076
  3.4 33.8 %all-to-all-start = ((f32[16,33,8,128]{3,2,1,0:T(8,128)}), f32[16,33,8,128]{3,2,1,0:T(8,128)S(1)}, u32[]{:S(2)}, u32[]{:S(2)}) async-start(f32[16,33,8,128]{3,2,1,0:T(8,128)} %shard_map.77), calls=%async_computation | async-start | bytes 4325376 | tf_op jit(solution)/shard_map/all_to_all | solution.py:318
  64.4 31.3 %collective-permute-start = (f32[512,512]{1,0:T(8,128)S(1)}, f32[512,512]{1,0:T(8,128)}, u32[]{:S(2)}, u32[]{:S(2)}) collective-permute-start(f32[512,512]{1,0:T(8,128)S(1)} %bitcast.15), channel_id=1, source_target_pairs={{0,224},{32,0},{64,32},{96,64},{128,96},{160,128},{192,160},{224,1... | collective-permute-start | bytes 3145736 | tf_op jit(solution)/shard_map/ppermute | solution.py:282
  70.3 26.1 %collective-permute-start.1 = (f32[512,512]{1,0:T(8,128)S(1)}, f32[512,512]{1,0:T(8,128)}, u32[]{:S(2)}, u32[]{:S(2)}) collective-permute-start(f32[512,512]{1,0:T(8,128)S(1)} %bitcast.16), channel_id=1, source_target_pairs={{0,32},{32,64},{64,96},{96,128},{128,160},{160,192},{192,224},{224... | collective-permute-start | bytes 3145736 | tf_op jit(solution)/shard_map/ppermute | solution.py:282
  71.9 3.2 %collective-permute-start.2 = (f32[2,8,1,32,256]{4,3,2,1,0:T(8,128)S(1)}, f32[2,8,1,32,256]{4,3,2,1,0:T(8,128)S(1)}, u32[]{:S(2)}, u32[]{:S(2)}) collective-permute-start(f32[2,8,1,32,256]{4,3,2,1,0:T(8,128)S(1)} %get-tuple-element.19), channel_id=1, source_target_pairs={{0,1},{1,0},{2,3},{3,2},{4,5},{5,4},{6,7},{7,6},{8,9},{9,8},{10,11... | collective-permute-start | bytes 1572872 | tf_op jit(solution)/shard_map/ppermute | solution.py:278
  72.9 16.5 %collective-permute-start.3 = (f32[256,512]{1,0:T(8,128)}, f32[256,512]{1,0:T(8,128)S(1)}, u32[]{:S(2)}, u32[]{:S(2)}) collective-permute-start(f32[256,512]{1,0:T(8,128)} %constant_dynamic-slice_fusion), channel_id=1, source_target_pairs={{0,16},{16,0},{1,17},{17,1},{2,18},{18,2},{3,19},{19,3},{4,20},{20... | collective-permute-start | bytes 1572872 | tf_op jit(solution)/shard_map/ppermute | solution.py:278
  76.0 19.7 %all-to-all-start.2 = ((f32[16,1,32,256]{3,2,1,0:T(8,128)}), f32[16,1,32,256]{3,2,1,0:T(8,128)S(1)}, u32[]{:S(2)}, u32[]{:S(2)}) async-start(f32[16,1,32,256]{3,2,1,0:T(8,128)} %bitcast.8), calls=%async_computation.2 | async-start | bytes 1048576 | tf_op jit(solution)/shard_map/all_to_all | solution.py:349
  100.5 2.8 %collective-permute-start.4 = (f32[2,8,2,32,256]{4,3,2,1,0:T(8,128)S(1)}, f32[2,8,2,32,256]{4,3,2,1,0:T(8,128)S(1)}, u32[]{:S(2)}, u32[]{:S(2)}) collective-permute-start(f32[2,8,2,32,256]{4,3,2,1,0:T(8,128)S(1)} %get-tuple-element.23), channel_id=1, source_target_pairs={{0,1},{1,0},{2,3},{3,2},{4,5},{5,4},{6,7},{7,6},{8,9},{9,8},{10,11... | collective-permute-start | bytes 3145736 | tf_op jit(solution)/shard_map/ppermute | solution.py:278
  100.6 26.0 %collective-permute-start.5 = (f32[512,512]{1,0:T(8,128)}, f32[512,512]{1,0:T(8,128)}, u32[]{:S(2)}, u32[]{:S(2)}) collective-permute-start(f32[512,512]{1,0:T(8,128)} %collective-permute-done.refs_1_), channel_id=1, source_target_pairs={{0,224},{32,0},{64,32},{96,64},{128,96},{160,128},{192,160},{224,1... | collective-permute-start | bytes 3145736 | tf_op jit(solution)/shard_map/ppermute | solution.py:282
  103.2 26.7 %collective-permute-start.6 = (f32[512,512]{1,0:T(8,128)}, f32[512,512]{1,0:T(8,128)}, u32[]{:S(2)}, u32[]{:S(2)}) collective-permute-start(f32[512,512]{1,0:T(8,128)} %collective-permute-done.1.refs_2_.refs_0_), channel_id=1, source_target_pairs={{0,32},{32,64},{64,96},{96,128},{128,160},{160,192},{192,224},{224... | collective-permute-start | bytes 3145736 | tf_op jit(solution)/shard_map/ppermute | solution.py:282
  104.4 25.5 %all-to-all-start.3 = ((f32[16,2,32,256]{3,2,1,0:T(8,128)}), f32[16,2,32,256]{3,2,1,0:T(8,128)S(1)}, u32[]{:S(2)}, u32[]{:S(2)}) async-start(f32[16,2,32,256]{3,2,1,0:T(8,128)} %bitcast.23), calls=%async_computation.3 | async-start | bytes 2097152 | tf_op jit(solution)/shard_map/all_to_all | solution.py:349
  134.4 2.7 %collective-permute-start.9 = (f32[2,8,2,32,256]{4,3,2,1,0:T(8,128)S(1)}, f32[2,8,2,32,256]{4,3,2,1,0:T(8,128)S(1)}, u32[]{:S(2)}, u32[]{:S(2)}) collective-permute-start(f32[2,8,2,32,256]{4,3,2,1,0:T(8,128)S(1)} %get-tuple-element.33), channel_id=1, source_target_pairs={{0,1},{1,0},{2,3},{3,2},{4,5},{5,4},{6,7},{7,6},{8,9},{9,8},{10,11... | collective-permute-start | bytes 3145736 | tf_op jit(solution)/shard_map/ppermute | solution.py:278
  138.3 22.5 %all-to-all-start.4 = ((f32[16,2,32,256]{3,2,1,0:T(8,128)}), f32[16,2,32,256]{3,2,1,0:T(8,128)S(1)}, u32[]{:S(2)}, u32[]{:S(2)}) async-start(f32[16,2,32,256]{3,2,1,0:T(8,128)} %bitcast.22), calls=%async_computation.4 | async-start | bytes 2097152 | tf_op jit(solution)/shard_map/all_to_all | solution.py:349
  145.1 20.4 %collective-permute-start.7 = (f32[2,32,256]{2,1,0:T(8,128)S(1)}, f32[2,32,256]{2,1,0:T(8,128)S(1)}, u32[]{:S(2)}, u32[]{:S(2)}) collective-permute-start(f32[2,32,256]{2,1,0:T(8,128)S(1)} %shard_map.83.d12), channel_id=1, source_target_pairs={{0,32},{1,48},{16,33},{17,49},{32,64},{33,80},{48,65},{49,81},{64,... | collective-permute-start | bytes 196616 | tf_op jit(solution)/shard_map/ppermute | solution.py:290
  145.2 20.3 %collective-permute-start.8 = (f32[1,32,256]{2,1,0:T(8,128)S(1)}, f32[1,32,256]{2,1,0:T(8,128)S(1)}, u32[]{:S(2)}, u32[]{:S(2)}) collective-permute-start(f32[1,32,256]{2,1,0:T(8,128)S(1)} %slice.13), channel_id=1, source_target_pairs={{0,224},{32,0},{64,32},{96,64},{128,96},{160,128},{192,160},{224,1... | collective-permute-start | bytes 98312 | tf_op jit(solution)/shard_map/ppermute | solution.py:282
  160.8 4.7 %collective-permute-start.10 = (f32[1,32,256]{2,1,0:T(8,128)S(1)}, f32[1,32,256]{2,1,0:T(8,128)S(1)}, u32[]{:S(2)}, u32[]{:S(2)}) collective-permute-start(f32[1,32,256]{2,1,0:T(8,128)S(1)} %get-tuple-element.37), channel_id=1, source_target_pairs={{0,224},{32,0},{64,32},{96,64},{128,96},{160,128},{192,160},{224,1... | collective-permute-start | bytes 98312 | tf_op jit(solution)/shard_map/ppermute | solution.py:282
  161.2 7.9 %collective-permute-start.11 = (f32[1,32,256]{2,1,0:T(8,128)S(1)}, f32[1,32,256]{2,1,0:T(8,128)S(1)}, u32[]{:S(2)}, u32[]{:S(2)}) collective-permute-start(f32[1,32,256]{2,1,0:T(8,128)S(1)} %get-tuple-element.37), channel_id=1, source_target_pairs={{0,64},{1,80},{16,65},{17,81},{32,96},{33,112},{48,97},{49,113},{6... | collective-permute-start | bytes 98312 | tf_op jit(solution)/shard_map/ppermute | solution.py:290
  161.5 7.6 %collective-permute-start.12 = (f32[1,32,256]{2,1,0:T(8,128)S(1)}, f32[1,32,256]{2,1,0:T(8,128)S(1)}, u32[]{:S(2)}, u32[]{:S(2)}) collective-permute-start(f32[1,32,256]{2,1,0:T(8,128)S(1)} %get-tuple-element.36), channel_id=1, source_target_pairs={{0,192},{32,224},{64,0},{96,32},{128,64},{160,96},{192,128},{224,1... | collective-permute-start | bytes 98312 | tf_op jit(solution)/shard_map/ppermute | solution.py:282

commit v3 on v2

--- a/solution.py
+++ b/solution.py
@@ -154,10 +154,11 @@
         hit = flat == cell - layer_of * (NY * NZ)
         source_ref[layer_of] = jnp.where(hit, SOURCE * weight_ref[layer_of, 6], 0.0)
         v = [got_ref[layer, k] for layer in range(LAYERS)]
-        update = None
+        update = [None] * LAYERS
         damping = 1.0 / ratio
         for sweep in range(SWEEPS):
-            misfit = []
+            newer = None if sweep == 0 else 1.0 / (2.0 * ratio - damping)
+            fresh = []
             for layer in range(LAYERS):
                 m = source_ref[layer] - v[layer]
                 if layer > 0:
@@ -166,15 +167,13 @@
                     m = m + weight_ref[layer, 1] * v[layer + 1]
                 for i, b in enumerate(beside(v[layer])):
                     m = m + weight_ref[layer, 2 + i] * b
-                misfit.append(m)
-            if sweep == 0:
-                update = [m * (1.0 / CENTRE) for m in misfit]
-            else:
-                newer = 1.0 / (2.0 * ratio - damping)
-                keep, add = newer * damping, 2.0 * newer / HALFWIDTH
-                update = [keep * u + add * m for u, m in zip(update, misfit)]
-                damping = newer
-            v = [a + u for a, u in zip(v, update)]
+                if sweep == 0:
+                    update[layer] = m * (1.0 / CENTRE)
+                else:
+                    update[layer] = newer * damping * update[layer] + 2.0 * newer / HALFWIDTH * m
+                fresh.append(v[layer] + update[layer])
+            damping = damping if sweep == 0 else newer
+            v = fresh
         h = [got_ref[layer, GROUP + k] for layer in range(LAYERS)]
         for layer in range(LAYERS):
             total = along_x(v, layer) * along_x(h, layer)
@@ -185,7 +184,7 @@
         source_ref[layer_of] = jnp.zeros((NY, NZ), F32)
         return carry
 
-    lax.fori_loop(0, GROUP, one, 0)
+    lax.fori_loop(0, GROUP, one, 0, unroll=4)
 
     def panel(layer, carry):
         for part in range(2):
@@ -218,17 +217,14 @@
     return pl.ds(pl.multiple_of(which * ROWS, ROWS), ROWS)
 
 
-def pair_kernel(pairs, me_ref, *refs):
-    blocks, (mine_ref, theirs_ref, high_ref, low_ref) = refs[:-4], refs[-4:]
+def pair_kernel(pairs, side, me_ref, *refs):
+    blocks, (out_ref, high_ref, low_ref) = refs[:-3], refs[-3:]
     for at, ref in enumerate(blocks):
         split_into(ref, high_ref, low_ref, at)
-    core = me_ref[2]
-    for side, out_ref in enumerate((mine_ref, theirs_ref)):
-        right = rows_of(side ^ core)
-        for i, (a, b) in enumerate(pairs):
-            for half in range(2):
-                block = product(high_ref, low_ref, (a, rows_of(half)), (b, right))
-                out_ref[half, :, i] = block.reshape(8, 32, ROWS)
+    right = rows_of(side ^ me_ref[2])
+    for i, (a, b) in enumerate(pairs):
+        block = product(high_ref, low_ref, a, (b, right))
+        out_ref[:, :, i] = block.reshape(2, 8, 32, ROWS)
 
 
 def sens_kernel(me_ref, panel_ref, got_ref, sens_ref):
@@ -254,9 +250,9 @@
     out_ref[...] = total
 
 
-def place_kernel(me_ref, d0, d12, up1, down1, far_down1, up2, down2, slot_ref):
+def place_kernel(me_ref, d0, d12, up1, down1, down2, far_up1, slot_ref):
     z = me_ref[3]
-    sources = (d0[0], d12[0], down1[0], far_down1[0], down2[0], up2[0], up1[1], up1[0])
+    sources = (d0[0], d12[0], down1[0], down2[0], down2[1], far_up1[0], up1[1], up1[0])
     for r, source in enumerate(sources):
         slot_ref[(z + r) % 8] = source
 
@@ -329,20 +325,22 @@
     )(me, obs_cell, got)
     x0 = lax.all_to_all(panel, ("xh",) + CELL_AXES, 0, 0, tiled=True).reshape(2 * ROWS, half)
     x1, xm = round_z(x0, -1), round_z(x0, 1)
-    other = swap(lax.dynamic_slice(x0, ((1 - xh) * ROWS, 0), (ROWS, half)), "xh")
     x2, xn = round_z(x1, -1), round_z(xm, 1)
 
     def partial(pairs, *blocks):
         count = len(pairs)
-        out = shape(2, 8, count, 32, ROWS)
-        mine, theirs = call(
-            functools.partial(pair_kernel, pairs),
-            (out, out),
-            [SMEM] + [VMEM] * len(blocks),
-            [pltpu.VMEM((len(blocks), 2 * ROWS, half), BF16)] * 2,
-            flops=24 * count * ROWS * ROWS * half, moved=2**23,
-        )(me, *blocks)
-        return mine + swap(theirs, "core")
+
+        def share(side):
+            return call(
+                functools.partial(pair_kernel, pairs, side),
+                shape(2, 8, count, 32, ROWS),
+                [SMEM] + [VMEM] * len(blocks),
+                [pltpu.VMEM((len(blocks), 2 * ROWS, half), BF16)] * 2,
+                flops=12 * count * ROWS * ROWS * half, moved=2**22,
+            )(me, *blocks)
+
+        theirs = swap(share(1), "core")
+        return share(0) + theirs
 
     def exchange(parts):
         parts = parts.reshape(16, parts.shape[2], 32, ROWS)
@@ -352,19 +350,21 @@
         return call(total_kernel, shape(*parts.shape[1:]), [VMEM])(parts)
 
     d0 = exchange(partial(((0, 0),), x0))
+    other = swap(lax.dynamic_slice(x0, ((1 - xh) * ROWS, 0), (ROWS, half)), "xh")
     x1, xm, d0, other = lax.optimization_barrier((x1, xm, d0, other))
     d12 = partial(((0, 1), (2, 1)), x0, x1, xm)
     d12, other = lax.optimization_barrier((d12, other))
     sens = call(sens_kernel, shape(ROWS * NY, NZ), [SMEM, VMEM, VMEM])(me, x0, other)
     d12 = exchange(d12)
     d12, x2, xn, sens = lax.optimization_barrier((d12, x2, xn, sens))
-    far = total(exchange(partial(((0, 1), (2, 1)), xm, x2, xn)))
     d0, d12 = total(d0), total(d12)
-
-    slots = call(place_kernel, shape(8, 32, ROWS), [SMEM] + [VMEM] * 7)(
-        me, d0, d12,
-        turn_z(d12, 1), round_z(d12[1:2], -1),
-        round_z(far[0:1], -1), turn_z(far[0:1], 2), round_z(far[1:2], -2),
+    up1, down1 = turn_z(d12, 1), round_z(d12[1:2], -1)
+    far = exchange(partial(((0, 1), (0, 2)), xn, x1, x2))
+    far, up1, down1 = lax.optimization_barrier((far, up1, down1))
+    far = total(far)
+
+    slots = call(place_kernel, shape(8, 32, ROWS), [SMEM] + [VMEM] * 6)(
+        me, d0, d12, up1, down1, round_z(far, -2), turn_z(far[0:1], 1)
     )
     block = lax.all_to_all(slots, ("y", "xl"), 0, 0, tiled=True)
     gram = call(finish_kernel, shape(ROWS, ROWS), [SMEM, VMEM])(me, block.reshape(ROWS, ROWS))

time: 184 us -> 180 us (0.978)
  waiting for transfers between devices: 79.3 us -> 68.8 us
  Pallas kernels: 23.2 us -> 29 us
    ppermute x4, waiting for transfers between devices: 10.1 us -> 5.04 us  [swap(): return lax.ppermute(x, axis, [(0, 1), (1, 0)])]
    ppermute x7 -> x6, waiting for transfers between devices: 17.7 us -> 12.8 us  [round_z(): return lax.ppermute(x, 'z', [(i, (i + by) % 8) for i in range(8)])]
    all_to_all x3, waiting for transfers between devices: 19.6 us -> 15.2 us  [exchange(): return lax.all_to_all(parts, PLANE, 0, 0, tiled=True)]
    pallas_call x4 -> x7, Pallas kernels: 10.7 us -> 14.8 us  [the longest x6 14.2 us: share(): call(functools.partial(pair_kernel, pairs, side), shape(2, 8, count, 32,...]
    ppermute x2, waiting for transfers between devices: 3.53 us -> 7.38 us  [turn_z(): return lax.ppermute(x, ('z', 'xh', 'core'), pairs)]
    pallas_call x3, Pallas kernels: 0.14 us -> 2.41 us  [total(): return call(total_kernel, shape(*parts.shape[1:]), [VMEM])(parts)]
    ppermute x7 -> x6, starting transfers between devices: 15.1 us -> 13.2 us  [round_z(): return lax.ppermute(x, 'z', [(i, (i + by) % 8) for i in range(8)])]
  transfers between devices with their start and end apart: 17 -> 16, of which waited for: 9 -> 9; matrix products, arithmetic and copies ran while one was open for 2% -> 2% of each run, Pallas kernels for 2% -> 8%
where the time goes in v3:
time: 180 us
  waiting for transfers between devices  68.8 us (38%)
  starting transfers between devices  43 us (24%)
  blocking collectives  32.8 us (18%)
  Pallas kernels  29 us (16%)
  other arithmetic  4.31 us (2%)
    all_to_all x1, waiting for transfers between devices, per_device(): got = lax.all_to_all(packed, CELL_AXES, 0, 0, tiled=True)  28.5 us
    all_to_all x1, blocking collectives, per_device(): lax.all_to_all(panel, ('xh',) + CELL_AXES, 0, 0, tiled=True)  20.6 us
    all_to_all x3, starting transfers between devices, exchange(): return lax.all_to_all(parts, PLANE, 0, 0, tiled=True)  20.3 us
    all_to_all x3, waiting for transfers between devices, exchange(): return lax.all_to_all(parts, PLANE, 0, 0, tiled=True)  15.2 us
    pallas_call x6, Pallas kernels, share(): call(functools.partial(pair_kernel, pairs, side), shape(2, 8, count, 32,...  14.2 us
    ppermute x6, starting transfers between devices, round_z(): return lax.ppermute(x, 'z', [(i, (i + by) % 8) for i in range(8)])  13.2 us
    ppermute x6, waiting for transfers between devices, round_z(): return lax.ppermute(x, 'z', [(i, (i + by) % 8) for i in range(8)])  12.8 us
    all_to_all x1, blocking collectives, per_device(): block = lax.all_to_all(slots, ('y', 'xl'), 0, 0, tiled=True)  12.2 us
  transfers between devices with their start and end apart: 16, of which 9 were waited for; matrix products, arithmetic and copies ran while one was open for 2% of the time, Pallas kernels for 8%

profile of v3, /device:TPU:4, one launch (start us, length us, event | category | flops | bytes accessed | tf_op | source)
XLA Modules:
  0.0 179.7 jit_solution(10189087238951977722)
XLA Ops:
  0.6 2.7 %shard_map.77 = f32[16,33,8,128]{3,2,1,0:T(8,128)} custom-call(f32[16]{0:T(128)} %logk_hbm.1, s32[256]{0:T(256)} %test_hbm.1, s32[1,8,128]{2,1,0:T(8,128)} %label_hbm.1, f32[16,16,8,128]{3,2,1,0:T(8,128)} %bitcast.26, f32[64,8,128]{2,1,0:T(8,128)} %bitcast.28), custom_call_target="tpu_custom_call" | custom-call | tf_op jit(solution)/shard_map/pallas_call | solution.py:296
  3.4 5.2 %all-to-all-start = ((f32[16,33,8,128]{3,2,1,0:T(8,128)}), f32[16,33,8,128]{3,2,1,0:T(8,128)S(1)}, u32[]{:S(2)}, u32[]{:S(2)}) async-start(f32[16,33,8,128]{3,2,1,0:T(8,128)} %shard_map.77), calls=%async_computation | async-start | bytes 4325376 | tf_op jit(solution)/shard_map/all_to_all | solution.py:314
  8.7 28.5 %all-to-all-done.got_ref = f32[16,33,8,128]{3,2,1,0:T(8,128)S(1)} async-done(((f32[16,33,8,128]{3,2,1,0:T(8,128)}), f32[16,33,8,128]{3,2,1,0:T(8,128)S(1)}, u32[]{:S(2)}, u32[]{:S(2)}) %all-to-all-start) | async-done | bytes 2162720 | tf_op jit(solution)/shard_map/all_to_all | solution.py:314
  37.2 5.5 %shard_map.78 = f32[32,16,512]{2,1,0:T(8,128)S(1)} custom-call(s32[8]{0:T(128)S(1)} %stack.30.me_ref, s32[256]{0:T(256)S(1)} %copy-done, f32[16,33,8,128]{3,2,1,0:T(8,128)S(1)} %all-to-all-done.got_ref), custom_call_target="tpu_custom_call" | custom-call | tf_op jit(solution)/shard_map/pallas_call | solution.py:316
  42.7 20.6 %all_to_all.30 = f32[32,16,512]{2,1,0:T(8,128)S(1)} all-to-all(f32[32,16,512]{2,1,0:T(8,128)S(1)} %shard_map.78), channel_id=1, replica_groups=mesh['z'=8,'xh'=2,'y'=4,'xl'=2,'core'=2] {'xh','y','xl','core'}, dimensions={0} | all-to-all | bytes 2097152 | tf_op jit(solution)/shard_map/all_to_all | solution.py:326
  65.2 3.9 %collective-permute-start = (f32[512,512]{1,0:T(8,128)S(1)}, f32[512,512]{1,0:T(8,128)S(1)}, u32[]{:S(2)}, u32[]{:S(2)}) collective-permute-start(f32[512,512]{1,0:T(8,128)S(1)} %bitcast.16), channel_id=1, source_target_pairs={{0,224},{32,0},{64,32},{96,64},{128,96},{160,128},{192,160},{224,1... | collective-permute-start | bytes 3145736 | tf_op jit(solution)/shard_map/ppermute | solution.py:278
  69.2 2.2 %shard_map.80 = f32[2,8,1,32,256]{4,3,2,1,0:T(8,128)} custom-call(s32[8]{0:T(128)S(1)} %stack.30.me_ref, f32[512,512]{1,0:T(8,128)S(1)} %bitcast.17), custom_call_target="tpu_custom_call" | custom-call | flops 402653184 | bytes 4194304 | tf_op jit(solution)/shard_map/pallas_call | solution.py:334
  72.2 2.2 %collective-permute-start.3 = (f32[256,512]{1,0:T(8,128)}, f32[256,512]{1,0:T(8,128)}, u32[]{:S(2)}, u32[]{:S(2)}) collective-permute-start(f32[256,512]{1,0:T(8,128)} %constant_dynamic-slice_fusion), channel_id=1, source_target_pairs={{0,16},{16,0},{1,17},{17,1},{2,18},{18,2},{3,19},{19,3},{4,20},{20... | collective-permute-start | bytes 1572872 | tf_op jit(solution)/shard_map/ppermute | solution.py:274
  77.8 6.0 %all-to-all-start.2 = ((f32[16,1,32,256]{3,2,1,0:T(8,128)}), f32[16,1,32,256]{3,2,1,0:T(8,128)}, u32[]{:S(2)}, u32[]{:S(2)}) async-start(f32[16,1,32,256]{3,2,1,0:T(8,128)} %bitcast.25), calls=%async_computation.2 | async-start | bytes 1048576 | tf_op jit(solution)/shard_map/all_to_all | solution.py:347
  83.8 5.0 %collective-permute-done.3.got_ref = f32[256,512]{1,0:T(8,128)} collective-permute-done((f32[256,512]{1,0:T(8,128)}, f32[256,512]{1,0:T(8,128)}, u32[]{:S(2)}, u32[]{:S(2)}) %collective-permute-start.3) | collective-permute-done | bytes 524320 | tf_op jit(solution)/shard_map/ppermute | solution.py:274
  88.8 6.3 %all-to-all-done.2.parts_ref = f32[16,1,32,256]{3,2,1,0:T(8,128)} async-done(((f32[16,1,32,256]{3,2,1,0:T(8,128)}), f32[16,1,32,256]{3,2,1,0:T(8,128)}, u32[]{:S(2)}, u32[]{:S(2)}) %all-to-all-start.2) | async-done | bytes 524320 | tf_op jit(solution)/shard_map/all_to_all | solution.py:347
  95.2 2.1 %shard_map.82 = f32[2,8,2,32,256]{4,3,2,1,0:T(8,128)S(1)} custom-call(s32[8]{0:T(128)S(1)} %stack.30.me_ref, f32[512,512]{1,0:T(8,128)S(1)} %bitcast.20, f32[512,512]{1,0:T(8,128)S(1)} %collective-permute-done.refs_1_, f32[512,512]{1,0:T(8,128)S(1)} %collective-permute-done.1.refs_2_), custom_call_target="tpu_custom_call" | custom-call | flops 805306368 | bytes 4194304 | tf_op jit(solution)/shard_map/pallas_call | solution.py:334
  97.5 3.2 %collective-permute-start.5 = (f32[512,512]{1,0:T(8,128)S(1)}, f32[512,512]{1,0:T(8,128)}, u32[]{:S(2)}, u32[]{:S(2)}) collective-permute-start(f32[512,512]{1,0:T(8,128)S(1)} %collective-permute-done.refs_1_), channel_id=1, source_target_pairs={{0,224},{32,0},{64,32},{96,64},{128,96},{160,128},{192,160},{224,1... | collective-permute-start | bytes 3145736 | tf_op jit(solution)/shard_map/ppermute | solution.py:278
  104.1 6.8 %all-to-all-start.3 = ((f32[16,2,32,256]{3,2,1,0:T(8,128)}), f32[16,2,32,256]{3,2,1,0:T(8,128)}, u32[]{:S(2)}, u32[]{:S(2)}) async-start(f32[16,2,32,256]{3,2,1,0:T(8,128)} %bitcast.24), calls=%async_computation.3 | async-start | bytes 2097152 | tf_op jit(solution)/shard_map/all_to_all | solution.py:347
  110.9 2.3 %shard_map.83 = f32[2048,128]{1,0:T(8,128)} custom-call(s32[8]{0:T(128)S(1)} %stack.30.me_ref, f32[512,512]{1,0:T(8,128)S(1)} %bitcast.22, f32[256,512]{1,0:T(8,128)} %collective-permute-done.3.got_ref), custom_call_target="tpu_custom_call" | custom-call | tf_op jit(solution)/shard_map/pallas_call | solution.py:357
  113.1 11.2 %collective-permute-done.6.refs_0_ = f32[512,512]{1,0:T(8,128)} collective-permute-done((f32[512,512]{1,0:T(8,128)S(1)}, f32[512,512]{1,0:T(8,128)}, u32[]{:S(2)}, u32[]{:S(2)}) %collective-permute-start.6) | collective-permute-done | bytes 1048608 | tf_op jit(solution)/shard_map/ppermute | solution.py:278
  125.7 3.2 %shard_map.87 = f32[2,8,2,32,256]{4,3,2,1,0:T(8,128)S(1)} custom-call(s32[8]{0:T(128)S(1)} %stack.30.me_ref, f32[512,512]{1,0:T(8,128)} %collective-permute-done.6.refs_0_, f32[512,512]{1,0:T(8,128)S(1)} %collective-permute-done.refs_1_, f32[512,512]{1,0:T(8,128)} %collective-permute-done.5.refs_2_), custom_call_target="tpu_custom_call" | custom-call | flops 805306368 | bytes 4194304 | tf_op jit(solution)/shard_map/pallas_call | solution.py:334
  129.0 3.2 %shard_map.86 = f32[2,8,2,32,256]{4,3,2,1,0:T(8,128)S(1)} custom-call(s32[8]{0:T(128)S(1)} %stack.30.me_ref, f32[512,512]{1,0:T(8,128)} %collective-permute-done.6.refs_0_, f32[512,512]{1,0:T(8,128)S(1)} %collective-permute-done.refs_1_, f32[512,512]{1,0:T(8,128)} %collective-permute-done.5.refs_2_), custom_call_target="tpu_custom_call" | custom-call | flops 805306368 | bytes 4194304 | tf_op jit(solution)/shard_map/pallas_call | solution.py:334
  133.3 7.5 %all-to-all-start.4 = ((f32[16,2,32,256]{3,2,1,0:T(8,128)}), f32[16,2,32,256]{3,2,1,0:T(8,128)S(1)}, u32[]{:S(2)}, u32[]{:S(2)}) async-start(f32[16,2,32,256]{3,2,1,0:T(8,128)} %bitcast.12), calls=%async_computation.4 | async-start | bytes 2097152 | tf_op jit(solution)/shard_map/all_to_all | solution.py:347
  142.2 2.6 %collective-permute-start.9 = (f32[1,32,256]{2,1,0:T(8,128)S(1)}, f32[1,32,256]{2,1,0:T(8,128)S(1)}, u32[]{:S(2)}, u32[]{:S(2)}) collective-permute-start(f32[1,32,256]{2,1,0:T(8,128)S(1)} %slice.8), channel_id=1, source_target_pairs={{0,224},{32,0},{64,32},{96,64},{128,96},{160,128},{192,160},{224,1... | collective-permute-start | bytes 98312 | tf_op jit(solution)/shard_map/ppermute | solution.py:278
  146.4 3.3 %collective-permute-done.8.up1 = f32[2,32,256]{2,1,0:T(8,128)S(1)} collective-permute-done((f32[2,32,256]{2,1,0:T(8,128)S(1)}, f32[2,32,256]{2,1,0:T(8,128)S(1)}, u32[]{:S(2)}, u32[]{:S(2)}) %collective-permute-start.8) | collective-permute-done | bytes 65568 | tf_op jit(solution)/shard_map/ppermute | solution.py:286
  149.7 7.5 %all-to-all-done.4.parts_ref = f32[16,2,32,256]{3,2,1,0:T(8,128)S(1)} async-done(((f32[16,2,32,256]{3,2,1,0:T(8,128)}), f32[16,2,32,256]{3,2,1,0:T(8,128)S(1)}, u32[]{:S(2)}, u32[]{:S(2)}) %all-to-all-start.4) | async-done | bytes 1048608 | tf_op jit(solution)/shard_map/all_to_all | solution.py:347
  161.5 4.1 %collective-permute-done.11.far_up1 = f32[1,32,256]{2,1,0:T(8,128)S(1)} collective-permute-done((f32[1,32,256]{2,1,0:T(8,128)S(1)}, f32[1,32,256]{2,1,0:T(8,128)S(1)}, u32[]{:S(2)}, u32[]{:S(2)}) %collective-permute-start.11) | collective-permute-done | bytes 32800 | tf_op jit(solution)/shard_map/ppermute | solution.py:286
  166.2 12.2 %all_to_all.31 = f32[8,32,256]{2,1,0:T(8,128)S(1)} all-to-all(f32[8,32,256]{2,1,0:T(8,128)S(1)} %shard_map.89), channel_id=1, replica_groups=mesh['z'=8,'xh'=2,'y'=4,'xl'=2,'core'=2] {'y','xl'}, dimensions={0} | all-to-all | bytes 524288 | tf_op jit(solution)/shard_map/all_to_all | solution.py:369
  (33 shorter events, 21.5 us)
Async XLA Ops:
  3.4 33.8 %copy-start = (s32[256]{0:T(256)S(1)}, s32[256]{0:T(256)}, u32[]{:S(2)}) copy-start(s32[256]{0:T(256)} %cell_ref.1) | copy-start | bytes 3076
  3.4 33.8 %all-to-all-start = ((f32[16,33,8,128]{3,2,1,0:T(8,128)}), f32[16,33,8,128]{3,2,1,0:T(8,128)S(1)}, u32[]{:S(2)}, u32[]{:S(2)}) async-start(f32[16,33,8,128]{3,2,1,0:T(8,128)} %shard_map.77), calls=%async_computation | async-start | bytes 4325376 | tf_op jit(solution)/shard_map/all_to_all | solution.py:314
  63.3 31.8 %collective-permute-start.1 = (f32[512,512]{1,0:T(8,128)S(1)}, f32[512,512]{1,0:T(8,128)S(1)}, u32[]{:S(2)}, u32[]{:S(2)}) collective-permute-start(f32[512,512]{1,0:T(8,128)S(1)} %bitcast.15), channel_id=1, source_target_pairs={{0,32},{32,64},{64,96},{96,128},{128,160},{160,192},{192,224},{224... | collective-permute-start | bytes 3145736 | tf_op jit(solution)/shard_map/ppermute | solution.py:278
  65.2 29.9 %collective-permute-start = (f32[512,512]{1,0:T(8,128)S(1)}, f32[512,512]{1,0:T(8,128)S(1)}, u32[]{:S(2)}, u32[]{:S(2)}) collective-permute-start(f32[512,512]{1,0:T(8,128)S(1)} %bitcast.16), channel_id=1, source_target_pairs={{0,224},{32,0},{64,32},{96,64},{128,96},{160,128},{192,160},{224,1... | collective-permute-start | bytes 3145736 | tf_op jit(solution)/shard_map/ppermute | solution.py:278
  71.4 4.5 %collective-permute-start.2 = (f32[2,8,1,32,256]{4,3,2,1,0:T(8,128)}, f32[2,8,1,32,256]{4,3,2,1,0:T(8,128)}, u32[]{:S(2)}, u32[]{:S(2)}) collective-permute-start(f32[2,8,1,32,256]{4,3,2,1,0:T(8,128)} %shard_map.80), channel_id=1, source_target_pairs={{0,1},{1,0},{2,3},{3,2},{4,5},{5,4},{6,7},{7,6},{8,9},{9,8},{10,11... | collective-permute-start | bytes 1572872 | tf_op jit(solution)/shard_map/ppermute | solution.py:274
  72.2 16.6 %collective-permute-start.3 = (f32[256,512]{1,0:T(8,128)}, f32[256,512]{1,0:T(8,128)}, u32[]{:S(2)}, u32[]{:S(2)}) collective-permute-start(f32[256,512]{1,0:T(8,128)} %constant_dynamic-slice_fusion), channel_id=1, source_target_pairs={{0,16},{16,0},{1,17},{17,1},{2,18},{18,2},{3,19},{19,3},{4,20},{20... | collective-permute-start | bytes 1572872 | tf_op jit(solution)/shard_map/ppermute | solution.py:274
  77.8 17.4 %all-to-all-start.2 = ((f32[16,1,32,256]{3,2,1,0:T(8,128)}), f32[16,1,32,256]{3,2,1,0:T(8,128)}, u32[]{:S(2)}, u32[]{:S(2)}) async-start(f32[16,1,32,256]{3,2,1,0:T(8,128)} %bitcast.25), calls=%async_computation.2 | async-start | bytes 1048576 | tf_op jit(solution)/shard_map/all_to_all | solution.py:347
  97.3 5.6 %collective-permute-start.4 = (f32[2,8,2,32,256]{4,3,2,1,0:T(8,128)S(1)}, f32[2,8,2,32,256]{4,3,2,1,0:T(8,128)S(1)}, u32[]{:S(2)}, u32[]{:S(2)}) collective-permute-start(f32[2,8,2,32,256]{4,3,2,1,0:T(8,128)S(1)} %shard_map.82), channel_id=1, source_target_pairs={{0,1},{1,0},{2,3},{3,2},{4,5},{5,4},{6,7},{7,6},{8,9},{9,8},{10,11... | collective-permute-start | bytes 3145736 | tf_op jit(solution)/shard_map/ppermute | solution.py:274
  97.4 26.9 %collective-permute-start.6 = (f32[512,512]{1,0:T(8,128)S(1)}, f32[512,512]{1,0:T(8,128)}, u32[]{:S(2)}, u32[]{:S(2)}) collective-permute-start(f32[512,512]{1,0:T(8,128)S(1)} %collective-permute-done.1.refs_2_), channel_id=1, source_target_pairs={{0,32},{32,64},{64,96},{96,128},{128,160},{160,192},{192,224},{224... | collective-permute-start | bytes 3145736 | tf_op jit(solution)/shard_map/ppermute | solution.py:278
  97.5 26.8 %collective-permute-start.5 = (f32[512,512]{1,0:T(8,128)S(1)}, f32[512,512]{1,0:T(8,128)}, u32[]{:S(2)}, u32[]{:S(2)}) collective-permute-start(f32[512,512]{1,0:T(8,128)S(1)} %collective-permute-done.refs_1_), channel_id=1, source_target_pairs={{0,224},{32,0},{64,32},{96,64},{128,96},{160,128},{192,160},{224,1... | collective-permute-start | bytes 3145736 | tf_op jit(solution)/shard_map/ppermute | solution.py:278
  104.1 21.6 %all-to-all-start.3 = ((f32[16,2,32,256]{3,2,1,0:T(8,128)}), f32[16,2,32,256]{3,2,1,0:T(8,128)}, u32[]{:S(2)}, u32[]{:S(2)}) async-start(f32[16,2,32,256]{3,2,1,0:T(8,128)} %bitcast.24), calls=%async_computation.3 | async-start | bytes 2097152 | tf_op jit(solution)/shard_map/all_to_all | solution.py:347
  128.9 3.3 %collective-permute-start.7 = (f32[2,8,2,32,256]{4,3,2,1,0:T(8,128)S(1)}, f32[2,8,2,32,256]{4,3,2,1,0:T(8,128)S(1)}, u32[]{:S(2)}, u32[]{:S(2)}) collective-permute-start(f32[2,8,2,32,256]{4,3,2,1,0:T(8,128)S(1)} %shard_map.87), channel_id=1, source_target_pairs={{0,1},{1,0},{2,3},{3,2},{4,5},{5,4},{6,7},{7,6},{8,9},{9,8},{10,11... | collective-permute-start | bytes 3145736 | tf_op jit(solution)/shard_map/ppermute | solution.py:274
  133.3 23.8 %all-to-all-start.4 = ((f32[16,2,32,256]{3,2,1,0:T(8,128)}), f32[16,2,32,256]{3,2,1,0:T(8,128)S(1)}, u32[]{:S(2)}, u32[]{:S(2)}) async-start(f32[16,2,32,256]{3,2,1,0:T(8,128)} %bitcast.12), calls=%async_computation.4 | async-start | bytes 2097152 | tf_op jit(solution)/shard_map/all_to_all | solution.py:347
  142.1 7.5 %collective-permute-start.8 = (f32[2,32,256]{2,1,0:T(8,128)S(1)}, f32[2,32,256]{2,1,0:T(8,128)S(1)}, u32[]{:S(2)}, u32[]{:S(2)}) collective-permute-start(f32[2,32,256]{2,1,0:T(8,128)S(1)} %shard_map.85.d12), channel_id=1, source_target_pairs={{0,32},{1,48},{16,33},{17,49},{32,64},{33,80},{48,65},{49,81},{64,... | collective-permute-start | bytes 196616 | tf_op jit(solution)/shard_map/ppermute | solution.py:286
  142.2 4.2 %collective-permute-start.9 = (f32[1,32,256]{2,1,0:T(8,128)S(1)}, f32[1,32,256]{2,1,0:T(8,128)S(1)}, u32[]{:S(2)}, u32[]{:S(2)}) collective-permute-start(f32[1,32,256]{2,1,0:T(8,128)S(1)} %slice.8), channel_id=1, source_target_pairs={{0,224},{32,0},{64,32},{96,64},{128,96},{160,128},{192,160},{224,1... | collective-permute-start | bytes 98312 | tf_op jit(solution)/shard_map/ppermute | solution.py:278
  157.2 8.4 %collective-permute-start.10 = (f32[2,32,256]{2,1,0:T(8,128)S(1)}, f32[2,32,256]{2,1,0:T(8,128)S(1)}, u32[]{:S(2)}, u32[]{:S(2)}) collective-permute-start(f32[2,32,256]{2,1,0:T(8,128)S(1)} %shard_map.88), channel_id=1, source_target_pairs={{0,192},{32,224},{64,0},{96,32},{128,64},{160,96},{192,128},{224,1... | collective-permute-start | bytes 196616 | tf_op jit(solution)/shard_map/ppermute | solution.py:278
  158.7 7.0 %collective-permute-start.11 = (f32[1,32,256]{2,1,0:T(8,128)S(1)}, f32[1,32,256]{2,1,0:T(8,128)S(1)}, u32[]{:S(2)}, u32[]{:S(2)}) collective-permute-start(f32[1,32,256]{2,1,0:T(8,128)S(1)} %slice.9), channel_id=1, source_target_pairs={{0,32},{1,48},{16,33},{17,49},{32,64},{33,80},{48,65},{49,81},{64,... | collective-permute-start | bytes 98312 | tf_op jit(solution)/shard_map/ppermute | solution.py:286

commit v4 on v3

--- a/solution.py
+++ b/solution.py
@@ -65,7 +65,7 @@
 
 def pack_kernel(
     logk_hbm, test_hbm, label_hbm, start_hbm, heads_hbm, packed_hbm,
-    logk_ref, test_ref, label_ref, heads_ref, packed_ref, sems,
+    logk_ref, test_ref, label_ref, heads_ref, start_ref, rest_ref, sems,
 ):
     moves = [
         pltpu.make_async_copy(source, target, sems.at[i])
@@ -74,7 +74,7 @@
             (test_hbm, test_ref),
             (logk_hbm, logk_ref),
             (label_hbm, label_ref),
-            (start_hbm, packed_ref.at[:, pl.ds(0, GROUP)]),
+            (start_hbm, start_ref),
         ))
     ]
     for move in moves:
@@ -88,18 +88,21 @@
     conduct = jnp.exp(logk)
     moves[0].wait()
     moves[1].wait()
+    moves[4].wait()
+    early = pltpu.make_async_copy(start_ref, packed_hbm.at[:, pl.ds(0, GROUP)], sems.at[5])
+    early.start()
 
     def one(target, carry):
         for k in range(GROUP):
-            packed_ref[target, GROUP + k] = heads_ref[test_ref[target * GROUP + k]]
-        packed_ref[target, 2 * GROUP] = conduct
+            rest_ref[target, k] = heads_ref[test_ref[target * GROUP + k]]
+        rest_ref[target, GROUP] = conduct
         return carry
 
     lax.fori_loop(0, LAYERS, one, 0)
-    moves[4].wait()
-    out = pltpu.make_async_copy(packed_ref, packed_hbm, sems.at[5])
-    out.start()
-    out.wait()
+    late = pltpu.make_async_copy(rest_ref, packed_hbm.at[:, pl.ds(GROUP, GROUP + 1)], sems.at[6])
+    late.start()
+    early.wait()
+    late.wait()
 
 
 def sweep_kernel(me_ref, cell_ref, got_ref, panel_ref, out_ref, weight_ref, source_ref):
@@ -303,8 +306,9 @@
             pltpu.SMEM((ROWS,), jnp.int32),
             pltpu.VMEM((1, NY, NZ), jnp.int32),
             pltpu.VMEM((TESTS, NY, NZ), F32),
-            pltpu.VMEM((LAYERS, 2 * GROUP + 1, NY, NZ), F32),
-            pltpu.SemaphoreType.DMA((6,)),
+            pltpu.VMEM((LAYERS, GROUP, NY, NZ), F32),
+            pltpu.VMEM((LAYERS, GROUP + 1, NY, NZ), F32),
+            pltpu.SemaphoreType.DMA((7,)),
         ],
         compiler_params=pltpu.CompilerParams(vmem_limit_bytes=60 * 2**20),
     )(

time: 180 us -> 180 us (level)
  no operation moved by 1% of the time
where the time goes in v4:
time: 180 us
  waiting for transfers between devices  68.8 us (38%)
  starting transfers between devices  43 us (24%)
  blocking collectives  32.8 us (18%)
  Pallas kernels  29 us (16%)
  other arithmetic  4.31 us (2%)
    all_to_all x1, waiting for transfers between devices, per_device(): got = lax.all_to_all(packed, CELL_AXES, 0, 0, tiled=True)  28.5 us
    all_to_all x1, blocking collectives, per_device(): lax.all_to_all(panel, ('xh',) + CELL_AXES, 0, 0, tiled=True)  20.6 us
    all_to_all x3, starting transfers between devices, exchange(): return lax.all_to_all(parts, PLANE, 0, 0, tiled=True)  20.3 us
    all_to_all x3, waiting for transfers between devices, exchange(): return lax.all_to_all(parts, PLANE, 0, 0, tiled=True)  15.2 us
    pallas_call x6, Pallas kernels, share(): call(functools.partial(pair_kernel, pairs, side), shape(2, 8, count, 32,...  14.2 us
    ppermute x6, starting transfers between devices, round_z(): return lax.ppermute(x, 'z', [(i, (i + by) % 8) for i in range(8)])  13.2 us
    ppermute x6, waiting for transfers between devices, round_z(): return lax.ppermute(x, 'z', [(i, (i + by) % 8) for i in range(8)])  12.8 us
    all_to_all x1, blocking collectives, per_device(): block = lax.all_to_all(slots, ('y', 'xl'), 0, 0, tiled=True)  12.2 us
  transfers between devices with their start and end apart: 16, of which 9 were waited for; matrix products, arithmetic and copies ran while one was open for 2% of the time, Pallas kernels for 8%

profile of v4, /device:TPU:4, one launch (start us, length us, event | category | flops | bytes accessed | tf_op | source)
XLA Modules:
  0.0 179.7 jit_solution(7384922409870410692)
XLA Ops:
  0.6 2.8 %shard_map.77 = f32[16,33,8,128]{3,2,1,0:T(8,128)} custom-call(f32[16]{0:T(128)} %logk_hbm.1, s32[256]{0:T(256)} %test_hbm.1, s32[1,8,128]{2,1,0:T(8,128)} %label_hbm.1, f32[16,16,8,128]{3,2,1,0:T(8,128)} %bitcast.26, f32[64,8,128]{2,1,0:T(8,128)} %bitcast.28), custom_call_target="tpu_custom_call" | custom-call | tf_op jit(solution)/shard_map/pallas_call | solution.py:299
  3.5 5.2 %all-to-all-start = ((f32[16,33,8,128]{3,2,1,0:T(8,128)}), f32[16,33,8,128]{3,2,1,0:T(8,128)S(1)}, u32[]{:S(2)}, u32[]{:S(2)}) async-start(f32[16,33,8,128]{3,2,1,0:T(8,128)} %shard_map.77), calls=%async_computation | async-start | bytes 4325376 | tf_op jit(solution)/shard_map/all_to_all | solution.py:318
  8.8 28.5 %all-to-all-done.got_ref = f32[16,33,8,128]{3,2,1,0:T(8,128)S(1)} async-done(((f32[16,33,8,128]{3,2,1,0:T(8,128)}), f32[16,33,8,128]{3,2,1,0:T(8,128)S(1)}, u32[]{:S(2)}, u32[]{:S(2)}) %all-to-all-start) | async-done | bytes 2162720 | tf_op jit(solution)/shard_map/all_to_all | solution.py:318
  37.3 5.5 %shard_map.78 = f32[32,16,512]{2,1,0:T(8,128)S(1)} custom-call(s32[8]{0:T(128)S(1)} %stack.30.me_ref, s32[256]{0:T(256)S(1)} %copy-done, f32[16,33,8,128]{3,2,1,0:T(8,128)S(1)} %all-to-all-done.got_ref), custom_call_target="tpu_custom_call" | custom-call | tf_op jit(solution)/shard_map/pallas_call | solution.py:320
  42.8 20.6 %all_to_all.30 = f32[32,16,512]{2,1,0:T(8,128)S(1)} all-to-all(f32[32,16,512]{2,1,0:T(8,128)S(1)} %shard_map.78), channel_id=1, replica_groups=mesh['z'=8,'xh'=2,'y'=4,'xl'=2,'core'=2] {'xh','y','xl','core'}, dimensions={0} | all-to-all | bytes 2097152 | tf_op jit(solution)/shard_map/all_to_all | solution.py:330
  65.3 3.9 %collective-permute-start = (f32[512,512]{1,0:T(8,128)S(1)}, f32[512,512]{1,0:T(8,128)S(1)}, u32[]{:S(2)}, u32[]{:S(2)}) collective-permute-start(f32[512,512]{1,0:T(8,128)S(1)} %bitcast.16), channel_id=1, source_target_pairs={{0,224},{32,0},{64,32},{96,64},{128,96},{160,128},{192,160},{224,1... | collective-permute-start | bytes 3145736 | tf_op jit(solution)/shard_map/ppermute | solution.py:281
  69.2 2.2 %shard_map.80 = f32[2,8,1,32,256]{4,3,2,1,0:T(8,128)} custom-call(s32[8]{0:T(128)S(1)} %stack.30.me_ref, f32[512,512]{1,0:T(8,128)S(1)} %bitcast.17), custom_call_target="tpu_custom_call" | custom-call | flops 402653184 | bytes 4194304 | tf_op jit(solution)/shard_map/pallas_call | solution.py:338
  72.2 2.2 %collective-permute-start.3 = (f32[256,512]{1,0:T(8,128)}, f32[256,512]{1,0:T(8,128)}, u32[]{:S(2)}, u32[]{:S(2)}) collective-permute-start(f32[256,512]{1,0:T(8,128)} %constant_dynamic-slice_fusion), channel_id=1, source_target_pairs={{0,16},{16,0},{1,17},{17,1},{2,18},{18,2},{3,19},{19,3},{4,20},{20... | collective-permute-start | bytes 1572872 | tf_op jit(solution)/shard_map/ppermute | solution.py:277
  77.8 6.0 %all-to-all-start.2 = ((f32[16,1,32,256]{3,2,1,0:T(8,128)}), f32[16,1,32,256]{3,2,1,0:T(8,128)}, u32[]{:S(2)}, u32[]{:S(2)}) async-start(f32[16,1,32,256]{3,2,1,0:T(8,128)} %bitcast.25), calls=%async_computation.2 | async-start | bytes 1048576 | tf_op jit(solution)/shard_map/all_to_all | solution.py:351
  83.9 5.0 %collective-permute-done.3.got_ref = f32[256,512]{1,0:T(8,128)} collective-permute-done((f32[256,512]{1,0:T(8,128)}, f32[256,512]{1,0:T(8,128)}, u32[]{:S(2)}, u32[]{:S(2)}) %collective-permute-start.3) | collective-permute-done | bytes 524320 | tf_op jit(solution)/shard_map/ppermute | solution.py:277
  88.9 6.3 %all-to-all-done.2.parts_ref = f32[16,1,32,256]{3,2,1,0:T(8,128)} async-done(((f32[16,1,32,256]{3,2,1,0:T(8,128)}), f32[16,1,32,256]{3,2,1,0:T(8,128)}, u32[]{:S(2)}, u32[]{:S(2)}) %all-to-all-start.2) | async-done | bytes 524320 | tf_op jit(solution)/shard_map/all_to_all | solution.py:351
  95.2 2.1 %shard_map.82 = f32[2,8,2,32,256]{4,3,2,1,0:T(8,128)S(1)} custom-call(s32[8]{0:T(128)S(1)} %stack.30.me_ref, f32[512,512]{1,0:T(8,128)S(1)} %bitcast.20, f32[512,512]{1,0:T(8,128)S(1)} %collective-permute-done.refs_1_, f32[512,512]{1,0:T(8,128)S(1)} %collective-permute-done.1.refs_2_), custom_call_target="tpu_custom_call" | custom-call | flops 805306368 | bytes 4194304 | tf_op jit(solution)/shard_map/pallas_call | solution.py:338
  97.6 3.2 %collective-permute-start.5 = (f32[512,512]{1,0:T(8,128)S(1)}, f32[512,512]{1,0:T(8,128)}, u32[]{:S(2)}, u32[]{:S(2)}) collective-permute-start(f32[512,512]{1,0:T(8,128)S(1)} %collective-permute-done.refs_1_), channel_id=1, source_target_pairs={{0,224},{32,0},{64,32},{96,64},{128,96},{160,128},{192,160},{224,1... | collective-permute-start | bytes 3145736 | tf_op jit(solution)/shard_map/ppermute | solution.py:281
  104.1 6.8 %all-to-all-start.3 = ((f32[16,2,32,256]{3,2,1,0:T(8,128)}), f32[16,2,32,256]{3,2,1,0:T(8,128)}, u32[]{:S(2)}, u32[]{:S(2)}) async-start(f32[16,2,32,256]{3,2,1,0:T(8,128)} %bitcast.24), calls=%async_computation.3 | async-start | bytes 2097152 | tf_op jit(solution)/shard_map/all_to_all | solution.py:351
  110.9 2.3 %shard_map.83 = f32[2048,128]{1,0:T(8,128)} custom-call(s32[8]{0:T(128)S(1)} %stack.30.me_ref, f32[512,512]{1,0:T(8,128)S(1)} %bitcast.22, f32[256,512]{1,0:T(8,128)} %collective-permute-done.3.got_ref), custom_call_target="tpu_custom_call" | custom-call | tf_op jit(solution)/shard_map/pallas_call | solution.py:361
  113.2 11.2 %collective-permute-done.6.refs_0_ = f32[512,512]{1,0:T(8,128)} collective-permute-done((f32[512,512]{1,0:T(8,128)S(1)}, f32[512,512]{1,0:T(8,128)}, u32[]{:S(2)}, u32[]{:S(2)}) %collective-permute-start.6) | collective-permute-done | bytes 1048608 | tf_op jit(solution)/shard_map/ppermute | solution.py:281
  125.7 3.2 %shard_map.87 = f32[2,8,2,32,256]{4,3,2,1,0:T(8,128)S(1)} custom-call(s32[8]{0:T(128)S(1)} %stack.30.me_ref, f32[512,512]{1,0:T(8,128)} %collective-permute-done.6.refs_0_, f32[512,512]{1,0:T(8,128)S(1)} %collective-permute-done.refs_1_, f32[512,512]{1,0:T(8,128)} %collective-permute-done.5.refs_2_), custom_call_target="tpu_custom_call" | custom-call | flops 805306368 | bytes 4194304 | tf_op jit(solution)/shard_map/pallas_call | solution.py:338
  129.0 3.2 %shard_map.86 = f32[2,8,2,32,256]{4,3,2,1,0:T(8,128)S(1)} custom-call(s32[8]{0:T(128)S(1)} %stack.30.me_ref, f32[512,512]{1,0:T(8,128)} %collective-permute-done.6.refs_0_, f32[512,512]{1,0:T(8,128)S(1)} %collective-permute-done.refs_1_, f32[512,512]{1,0:T(8,128)} %collective-permute-done.5.refs_2_), custom_call_target="tpu_custom_call" | custom-call | flops 805306368 | bytes 4194304 | tf_op jit(solution)/shard_map/pallas_call | solution.py:338
  133.4 7.5 %all-to-all-start.4 = ((f32[16,2,32,256]{3,2,1,0:T(8,128)}), f32[16,2,32,256]{3,2,1,0:T(8,128)S(1)}, u32[]{:S(2)}, u32[]{:S(2)}) async-start(f32[16,2,32,256]{3,2,1,0:T(8,128)} %bitcast.12), calls=%async_computation.4 | async-start | bytes 2097152 | tf_op jit(solution)/shard_map/all_to_all | solution.py:351
  142.3 2.6 %collective-permute-start.9 = (f32[1,32,256]{2,1,0:T(8,128)S(1)}, f32[1,32,256]{2,1,0:T(8,128)S(1)}, u32[]{:S(2)}, u32[]{:S(2)}) collective-permute-start(f32[1,32,256]{2,1,0:T(8,128)S(1)} %slice.8), channel_id=1, source_target_pairs={{0,224},{32,0},{64,32},{96,64},{128,96},{160,128},{192,160},{224,1... | collective-permute-start | bytes 98312 | tf_op jit(solution)/shard_map/ppermute | solution.py:281
  146.5 3.3 %collective-permute-done.8.up1 = f32[2,32,256]{2,1,0:T(8,128)S(1)} collective-permute-done((f32[2,32,256]{2,1,0:T(8,128)S(1)}, f32[2,32,256]{2,1,0:T(8,128)S(1)}, u32[]{:S(2)}, u32[]{:S(2)}) %collective-permute-start.8) | collective-permute-done | bytes 65568 | tf_op jit(solution)/shard_map/ppermute | solution.py:289
  149.7 7.5 %all-to-all-done.4.parts_ref = f32[16,2,32,256]{3,2,1,0:T(8,128)S(1)} async-done(((f32[16,2,32,256]{3,2,1,0:T(8,128)}), f32[16,2,32,256]{3,2,1,0:T(8,128)S(1)}, u32[]{:S(2)}, u32[]{:S(2)}) %all-to-all-start.4) | async-done | bytes 1048608 | tf_op jit(solution)/shard_map/all_to_all | solution.py:351
  161.6 4.1 %collective-permute-done.11.far_up1 = f32[1,32,256]{2,1,0:T(8,128)S(1)} collective-permute-done((f32[1,32,256]{2,1,0:T(8,128)S(1)}, f32[1,32,256]{2,1,0:T(8,128)S(1)}, u32[]{:S(2)}, u32[]{:S(2)}) %collective-permute-start.11) | collective-permute-done | bytes 32800 | tf_op jit(solution)/shard_map/ppermute | solution.py:289
  166.3 12.2 %all_to_all.31 = f32[8,32,256]{2,1,0:T(8,128)S(1)} all-to-all(f32[8,32,256]{2,1,0:T(8,128)S(1)} %shard_map.89), channel_id=1, replica_groups=mesh['z'=8,'xh'=2,'y'=4,'xl'=2,'core'=2] {'y','xl'}, dimensions={0} | all-to-all | bytes 524288 | tf_op jit(solution)/shard_map/all_to_all | solution.py:373
  (33 shorter events, 21.5 us)
Async XLA Ops:
  3.4 33.8 %copy-start = (s32[256]{0:T(256)S(1)}, s32[256]{0:T(256)}, u32[]{:S(2)}) copy-start(s32[256]{0:T(256)} %cell_ref.1) | copy-start | bytes 3076
  3.5 33.8 %all-to-all-start = ((f32[16,33,8,128]{3,2,1,0:T(8,128)}), f32[16,33,8,128]{3,2,1,0:T(8,128)S(1)}, u32[]{:S(2)}, u32[]{:S(2)}) async-start(f32[16,33,8,128]{3,2,1,0:T(8,128)} %shard_map.77), calls=%async_computation | async-start | bytes 4325376 | tf_op jit(solution)/shard_map/all_to_all | solution.py:318
  63.4 31.8 %collective-permute-start.1 = (f32[512,512]{1,0:T(8,128)S(1)}, f32[512,512]{1,0:T(8,128)S(1)}, u32[]{:S(2)}, u32[]{:S(2)}) collective-permute-start(f32[512,512]{1,0:T(8,128)S(1)} %bitcast.15), channel_id=1, source_target_pairs={{0,32},{32,64},{64,96},{96,128},{128,160},{160,192},{192,224},{224... | collective-permute-start | bytes 3145736 | tf_op jit(solution)/shard_map/ppermute | solution.py:281
  65.3 29.9 %collective-permute-start = (f32[512,512]{1,0:T(8,128)S(1)}, f32[512,512]{1,0:T(8,128)S(1)}, u32[]{:S(2)}, u32[]{:S(2)}) collective-permute-start(f32[512,512]{1,0:T(8,128)S(1)} %bitcast.16), channel_id=1, source_target_pairs={{0,224},{32,0},{64,32},{96,64},{128,96},{160,128},{192,160},{224,1... | collective-permute-start | bytes 3145736 | tf_op jit(solution)/shard_map/ppermute | solution.py:281
  71.4 4.5 %collective-permute-start.2 = (f32[2,8,1,32,256]{4,3,2,1,0:T(8,128)}, f32[2,8,1,32,256]{4,3,2,1,0:T(8,128)}, u32[]{:S(2)}, u32[]{:S(2)}) collective-permute-start(f32[2,8,1,32,256]{4,3,2,1,0:T(8,128)} %shard_map.80), channel_id=1, source_target_pairs={{0,1},{1,0},{2,3},{3,2},{4,5},{5,4},{6,7},{7,6},{8,9},{9,8},{10,11... | collective-permute-start | bytes 1572872 | tf_op jit(solution)/shard_map/ppermute | solution.py:277
  72.2 16.6 %collective-permute-start.3 = (f32[256,512]{1,0:T(8,128)}, f32[256,512]{1,0:T(8,128)}, u32[]{:S(2)}, u32[]{:S(2)}) collective-permute-start(f32[256,512]{1,0:T(8,128)} %constant_dynamic-slice_fusion), channel_id=1, source_target_pairs={{0,16},{16,0},{1,17},{17,1},{2,18},{18,2},{3,19},{19,3},{4,20},{20... | collective-permute-start | bytes 1572872 | tf_op jit(solution)/shard_map/ppermute | solution.py:277
  77.8 17.4 %all-to-all-start.2 = ((f32[16,1,32,256]{3,2,1,0:T(8,128)}), f32[16,1,32,256]{3,2,1,0:T(8,128)}, u32[]{:S(2)}, u32[]{:S(2)}) async-start(f32[16,1,32,256]{3,2,1,0:T(8,128)} %bitcast.25), calls=%async_computation.2 | async-start | bytes 1048576 | tf_op jit(solution)/shard_map/all_to_all | solution.py:351
  97.4 5.6 %collective-permute-start.4 = (f32[2,8,2,32,256]{4,3,2,1,0:T(8,128)S(1)}, f32[2,8,2,32,256]{4,3,2,1,0:T(8,128)S(1)}, u32[]{:S(2)}, u32[]{:S(2)}) collective-permute-start(f32[2,8,2,32,256]{4,3,2,1,0:T(8,128)S(1)} %shard_map.82), channel_id=1, source_target_pairs={{0,1},{1,0},{2,3},{3,2},{4,5},{5,4},{6,7},{7,6},{8,9},{9,8},{10,11... | collective-permute-start | bytes 3145736 | tf_op jit(solution)/shard_map/ppermute | solution.py:277
  97.5 26.9 %collective-permute-start.6 = (f32[512,512]{1,0:T(8,128)S(1)}, f32[512,512]{1,0:T(8,128)}, u32[]{:S(2)}, u32[]{:S(2)}) collective-permute-start(f32[512,512]{1,0:T(8,128)S(1)} %collective-permute-done.1.refs_2_), channel_id=1, source_target_pairs={{0,32},{32,64},{64,96},{96,128},{128,160},{160,192},{192,224},{224... | collective-permute-start | bytes 3145736 | tf_op jit(solution)/shard_map/ppermute | solution.py:281
  97.6 26.8 %collective-permute-start.5 = (f32[512,512]{1,0:T(8,128)S(1)}, f32[512,512]{1,0:T(8,128)}, u32[]{:S(2)}, u32[]{:S(2)}) collective-permute-start(f32[512,512]{1,0:T(8,128)S(1)} %collective-permute-done.refs_1_), channel_id=1, source_target_pairs={{0,224},{32,0},{64,32},{96,64},{128,96},{160,128},{192,160},{224,1... | collective-permute-start | bytes 3145736 | tf_op jit(solution)/shard_map/ppermute | solution.py:281
  104.1 21.6 %all-to-all-start.3 = ((f32[16,2,32,256]{3,2,1,0:T(8,128)}), f32[16,2,32,256]{3,2,1,0:T(8,128)}, u32[]{:S(2)}, u32[]{:S(2)}) async-start(f32[16,2,32,256]{3,2,1,0:T(8,128)} %bitcast.24), calls=%async_computation.3 | async-start | bytes 2097152 | tf_op jit(solution)/shard_map/all_to_all | solution.py:351
  128.9 3.3 %collective-permute-start.7 = (f32[2,8,2,32,256]{4,3,2,1,0:T(8,128)S(1)}, f32[2,8,2,32,256]{4,3,2,1,0:T(8,128)S(1)}, u32[]{:S(2)}, u32[]{:S(2)}) collective-permute-start(f32[2,8,2,32,256]{4,3,2,1,0:T(8,128)S(1)} %shard_map.87), channel_id=1, source_target_pairs={{0,1},{1,0},{2,3},{3,2},{4,5},{5,4},{6,7},{7,6},{8,9},{9,8},{10,11... | collective-permute-start | bytes 3145736 | tf_op jit(solution)/shard_map/ppermute | solution.py:277
  133.4 23.8 %all-to-all-start.4 = ((f32[16,2,32,256]{3,2,1,0:T(8,128)}), f32[16,2,32,256]{3,2,1,0:T(8,128)S(1)}, u32[]{:S(2)}, u32[]{:S(2)}) async-start(f32[16,2,32,256]{3,2,1,0:T(8,128)} %bitcast.12), calls=%async_computation.4 | async-start | bytes 2097152 | tf_op jit(solution)/shard_map/all_to_all | solution.py:351
  142.2 7.5 %collective-permute-start.8 = (f32[2,32,256]{2,1,0:T(8,128)S(1)}, f32[2,32,256]{2,1,0:T(8,128)S(1)}, u32[]{:S(2)}, u32[]{:S(2)}) collective-permute-start(f32[2,32,256]{2,1,0:T(8,128)S(1)} %shard_map.85.d12), channel_id=1, source_target_pairs={{0,32},{1,48},{16,33},{17,49},{32,64},{33,80},{48,65},{49,81},{64,... | collective-permute-start | bytes 196616 | tf_op jit(solution)/shard_map/ppermute | solution.py:289
  142.3 4.2 %collective-permute-start.9 = (f32[1,32,256]{2,1,0:T(8,128)S(1)}, f32[1,32,256]{2,1,0:T(8,128)S(1)}, u32[]{:S(2)}, u32[]{:S(2)}) collective-permute-start(f32[1,32,256]{2,1,0:T(8,128)S(1)} %slice.8), channel_id=1, source_target_pairs={{0,224},{32,0},{64,32},{96,64},{128,96},{160,128},{192,160},{224,1... | collective-permute-start | bytes 98312 | tf_op jit(solution)/shard_map/ppermute | solution.py:281
  157.3 8.4 %collective-permute-start.10 = (f32[2,32,256]{2,1,0:T(8,128)S(1)}, f32[2,32,256]{2,1,0:T(8,128)S(1)}, u32[]{:S(2)}, u32[]{:S(2)}) collective-permute-start(f32[2,32,256]{2,1,0:T(8,128)S(1)} %shard_map.88), channel_id=1, source_target_pairs={{0,192},{32,224},{64,0},{96,32},{128,64},{160,96},{192,128},{224,1... | collective-permute-start | bytes 196616 | tf_op jit(solution)/shard_map/ppermute | solution.py:281
  158.7 7.0 %collective-permute-start.11 = (f32[1,32,256]{2,1,0:T(8,128)S(1)}, f32[1,32,256]{2,1,0:T(8,128)S(1)}, u32[]{:S(2)}, u32[]{:S(2)}) collective-permute-start(f32[1,32,256]{2,1,0:T(8,128)S(1)} %slice.9), channel_id=1, source_target_pairs={{0,32},{1,48},{16,33},{17,49},{32,64},{33,80},{48,65},{49,81},{64,... | collective-permute-start | bytes 98312 | tf_op jit(solution)/shard_map/ppermute | solution.py:289

commit v5 on v3

--- a/solution.py
+++ b/solution.py
@@ -350,23 +350,22 @@
         return call(total_kernel, shape(*parts.shape[1:]), [VMEM])(parts)
 
     d0 = exchange(partial(((0, 0),), x0))
-    other = swap(lax.dynamic_slice(x0, ((1 - xh) * ROWS, 0), (ROWS, half)), "xh")
+    other = lax.dynamic_slice(x0, ((1 - xh) * ROWS, 0), (ROWS, half))
     x1, xm, d0, other = lax.optimization_barrier((x1, xm, d0, other))
-    d12 = partial(((0, 1), (2, 1)), x0, x1, xm)
-    d12, other = lax.optimization_barrier((d12, other))
-    sens = call(sens_kernel, shape(ROWS * NY, NZ), [SMEM, VMEM, VMEM])(me, x0, other)
-    d12 = exchange(d12)
-    d12, x2, xn, sens = lax.optimization_barrier((d12, x2, xn, sens))
+    d12 = exchange(partial(((0, 1), (2, 1)), x0, x1, xm))
+    d12, x2, xn = lax.optimization_barrier((d12, x2, xn))
     d0, d12 = total(d0), total(d12)
     up1, down1 = turn_z(d12, 1), round_z(d12[1:2], -1)
     far = exchange(partial(((0, 1), (0, 2)), xn, x1, x2))
-    far, up1, down1 = lax.optimization_barrier((far, up1, down1))
+    far, up1, down1, other = lax.optimization_barrier((far, up1, down1, other))
     far = total(far)
+    sens = call(sens_kernel, shape(ROWS * NY, NZ), [SMEM, VMEM, VMEM])(me, x0, swap(other, "xh"))
 
     slots = call(place_kernel, shape(8, 32, ROWS), [SMEM] + [VMEM] * 6)(
         me, d0, d12, up1, down1, round_z(far, -2), turn_z(far[0:1], 1)
     )
     block = lax.all_to_all(slots, ("y", "xl"), 0, 0, tiled=True)
+    block, sens = lax.optimization_barrier((block, sens))
     gram = call(finish_kernel, shape(ROWS, ROWS), [SMEM, VMEM])(me, block.reshape(ROWS, ROWS))
     return sens.reshape(ROWS, 1, NY, NZ), gram
 

time: 180 us -> 181 us (level)
  waiting for transfers between devices: 68.8 us -> 81.8 us
  blocking collectives: 32.8 us -> 20.6 us
    all_to_all x1 -> x0, blocking collectives: 12.2 us -> none  [per_device(): block = lax.all_to_all(slots, ('y', 'xl'), 0, 0, tiled=True)]
    ppermute x6, waiting for transfers between devices: 12.8 us -> 22.2 us  [round_z(): return lax.ppermute(x, 'z', [(i, (i + by) % 8) for i in range(8)])]
    all_to_all x0 -> x1, waiting for transfers between devices: none -> 5.54 us  [per_device(): block = lax.all_to_all(slots, ('y', 'xl'), 0, 0, tiled=True)]
    ppermute x4, waiting for transfers between devices: 5.04 us -> 0.51 us  [swap(): return lax.ppermute(x, axis, [(0, 1), (1, 0)])]
    all_to_all x0 -> x1, starting transfers between devices: none -> 3.71 us  [per_device(): block = lax.all_to_all(slots, ('y', 'xl'), 0, 0, tiled=True)]
    ppermute x6, starting transfers between devices: 13.2 us -> 10.8 us  [round_z(): return lax.ppermute(x, 'z', [(i, (i + by) % 8) for i in range(8)])]
  transfers between devices with their start and end apart: 16 -> 17, of which waited for: 9 -> 13; matrix products, arithmetic and copies ran while one was open for 2% -> 2% of each run, Pallas kernels for 8% -> 8%
where the time goes in v5:
time: 181 us; the launch traced here: 180 us
  waiting for transfers between devices  81.8 us (45%)
  starting transfers between devices  44.1 us (24%)
  Pallas kernels  28.3 us (16%)
  blocking collectives  20.6 us (11%)
  other arithmetic  3.2 us (2%)
    all_to_all x1, waiting for transfers between devices, per_device(): got = lax.all_to_all(packed, CELL_AXES, 0, 0, tiled=True)  28.5 us
    ppermute x6, waiting for transfers between devices, round_z(): return lax.ppermute(x, 'z', [(i, (i + by) % 8) for i in range(8)])  22.2 us
    all_to_all x1, blocking collectives, per_device(): lax.all_to_all(panel, ('xh',) + CELL_AXES, 0, 0, tiled=True)  20.6 us
    all_to_all x3, starting transfers between devices, exchange(): return lax.all_to_all(parts, PLANE, 0, 0, tiled=True)  20.1 us
    all_to_all x3, waiting for transfers between devices, exchange(): return lax.all_to_all(parts, PLANE, 0, 0, tiled=True)  16.7 us
    pallas_call x6, Pallas kernels, share(): call(functools.partial(pair_kernel, pairs, side), shape(2, 8, count, 32,...  13.4 us
    ppermute x6, starting transfers between devices, round_z(): return lax.ppermute(x, 'z', [(i, (i + by) % 8) for i in range(8)])  10.8 us
    ppermute x2, waiting for transfers between devices, turn_z(): return lax.ppermute(x, ('z', 'xh', 'core'), pairs)  8.41 us
  transfers between devices with their start and end apart: 17, of which 13 were waited for; matrix products, arithmetic and copies ran while one was open for 2% of the time, Pallas kernels for 8%

profile of v5, /device:TPU:4, one launch (start us, length us, event | category | flops | bytes accessed | tf_op | source)
XLA Modules:
  0.0 179.8 jit_solution(5921753385837494571)
XLA Ops:
  0.6 2.7 %shard_map.77 = f32[16,33,8,128]{3,2,1,0:T(8,128)} custom-call(f32[16]{0:T(128)} %logk_hbm.1, s32[256]{0:T(256)} %test_hbm.1, s32[1,8,128]{2,1,0:T(8,128)} %label_hbm.1, f32[16,16,8,128]{3,2,1,0:T(8,128)} %bitcast.27, f32[64,8,128]{2,1,0:T(8,128)} %bitcast.29), custom_call_target="tpu_custom_call" | custom-call | tf_op jit(solution)/shard_map/pallas_call | solution.py:296
  3.4 5.2 %all-to-all-start = ((f32[16,33,8,128]{3,2,1,0:T(8,128)}), f32[16,33,8,128]{3,2,1,0:T(8,128)S(1)}, u32[]{:S(2)}, u32[]{:S(2)}) async-start(f32[16,33,8,128]{3,2,1,0:T(8,128)} %shard_map.77), calls=%async_computation | async-start | bytes 4325376 | tf_op jit(solution)/shard_map/all_to_all | solution.py:314
  8.7 28.5 %all-to-all-done.got_ref = f32[16,33,8,128]{3,2,1,0:T(8,128)S(1)} async-done(((f32[16,33,8,128]{3,2,1,0:T(8,128)}), f32[16,33,8,128]{3,2,1,0:T(8,128)S(1)}, u32[]{:S(2)}, u32[]{:S(2)}) %all-to-all-start) | async-done | bytes 2162720 | tf_op jit(solution)/shard_map/all_to_all | solution.py:314
  37.2 5.5 %shard_map.78 = f32[32,16,512]{2,1,0:T(8,128)S(1)} custom-call(s32[8]{0:T(128)S(1)} %stack.30.me_ref, s32[256]{0:T(256)S(1)} %copy-done, f32[16,33,8,128]{3,2,1,0:T(8,128)S(1)} %all-to-all-done.got_ref), custom_call_target="tpu_custom_call" | custom-call | tf_op jit(solution)/shard_map/pallas_call | solution.py:316
  42.7 20.6 %all_to_all.30 = f32[32,16,512]{2,1,0:T(8,128)S(1)} all-to-all(f32[32,16,512]{2,1,0:T(8,128)S(1)} %shard_map.78), channel_id=1, replica_groups=mesh['z'=8,'xh'=2,'y'=4,'xl'=2,'core'=2] {'xh','y','xl','core'}, dimensions={0} | all-to-all | bytes 2097152 | tf_op jit(solution)/shard_map/all_to_all | solution.py:326
  63.3 5.9 %collective-permute-start = (f32[512,512]{1,0:T(8,128)S(1)}, f32[512,512]{1,0:T(8,128)S(1)}, u32[]{:S(2)}, u32[]{:S(2)}) collective-permute-start(f32[512,512]{1,0:T(8,128)S(1)} %bitcast.15), channel_id=1, source_target_pairs={{0,224},{32,0},{64,32},{96,64},{128,96},{160,128},{192,160},{224,1... | collective-permute-start | bytes 3145736 | tf_op jit(solution)/shard_map/ppermute | solution.py:278
  73.4 6.3 %all-to-all-start.2 = ((f32[16,1,32,256]{3,2,1,0:T(8,128)}), f32[16,1,32,256]{3,2,1,0:T(8,128)}, u32[]{:S(2)}, u32[]{:S(2)}) async-start(f32[16,1,32,256]{3,2,1,0:T(8,128)} %bitcast.26), calls=%async_computation.2 | async-start | bytes 1048576 | tf_op jit(solution)/shard_map/all_to_all | solution.py:347
  80.5 9.1 %all-to-all-done.2.parts_ref = f32[16,1,32,256]{3,2,1,0:T(8,128)} async-done(((f32[16,1,32,256]{3,2,1,0:T(8,128)}), f32[16,1,32,256]{3,2,1,0:T(8,128)}, u32[]{:S(2)}, u32[]{:S(2)}) %all-to-all-start.2) | async-done | bytes 524320 | tf_op jit(solution)/shard_map/all_to_all | solution.py:347
  89.6 2.1 %collective-permute-done.refs_1_ = f32[512,512]{1,0:T(8,128)S(1)} collective-permute-done((f32[512,512]{1,0:T(8,128)S(1)}, f32[512,512]{1,0:T(8,128)S(1)}, u32[]{:S(2)}, u32[]{:S(2)}) %collective-permute-start) | collective-permute-done | bytes 1048608 | tf_op jit(solution)/shard_map/ppermute | solution.py:278
  91.8 3.4 %collective-permute-done.1.refs_2_ = f32[512,512]{1,0:T(8,128)S(1)} collective-permute-done((f32[512,512]{1,0:T(8,128)S(1)}, f32[512,512]{1,0:T(8,128)S(1)}, u32[]{:S(2)}, u32[]{:S(2)}) %collective-permute-start.1) | collective-permute-done | bytes 1048608 | tf_op jit(solution)/shard_map/ppermute | solution.py:278
  95.2 2.1 %shard_map.83 = f32[2,8,2,32,256]{4,3,2,1,0:T(8,128)S(1)} custom-call(s32[8]{0:T(128)S(1)} %stack.30.me_ref, f32[512,512]{1,0:T(8,128)S(1)} %bitcast.20, f32[512,512]{1,0:T(8,128)S(1)} %collective-permute-done.refs_1_, f32[512,512]{1,0:T(8,128)S(1)} %collective-permute-done.1.refs_2_), custom_call_target="tpu_custom_call" | custom-call | flops 805306368 | bytes 4194304 | tf_op jit(solution)/shard_map/pallas_call | solution.py:334
  99.5 2.1 %shard_map.82 = f32[2,8,2,32,256]{4,3,2,1,0:T(8,128)S(1)} custom-call(s32[8]{0:T(128)S(1)} %stack.30.me_ref, f32[512,512]{1,0:T(8,128)S(1)} %bitcast.21, f32[512,512]{1,0:T(8,128)S(1)} %collective-permute-done.refs_1_, f32[512,512]{1,0:T(8,128)S(1)} %collective-permute-done.1.refs_2_), custom_call_target="tpu_custom_call" | custom-call | flops 805306368 | bytes 4194304 | tf_op jit(solution)/shard_map/pallas_call | solution.py:334
  102.8 6.5 %all-to-all-start.3 = ((f32[16,2,32,256]{3,2,1,0:T(8,128)}), f32[16,2,32,256]{3,2,1,0:T(8,128)}, u32[]{:S(2)}, u32[]{:S(2)}) async-start(f32[16,2,32,256]{3,2,1,0:T(8,128)} %bitcast.25), calls=%async_computation.3 | async-start | bytes 2097152 | tf_op jit(solution)/shard_map/all_to_all | solution.py:347
  109.3 13.8 %collective-permute-done.4.refs_2_ = f32[512,512]{1,0:T(8,128)} collective-permute-done((f32[512,512]{1,0:T(8,128)S(1)}, f32[512,512]{1,0:T(8,128)}, u32[]{:S(2)}, u32[]{:S(2)}) %collective-permute-start.4) | collective-permute-done | bytes 1048608 | tf_op jit(solution)/shard_map/ppermute | solution.py:278
  124.5 3.2 %shard_map.86 = f32[2,8,2,32,256]{4,3,2,1,0:T(8,128)S(1)} custom-call(s32[8]{0:T(128)S(1)} %stack.30.me_ref, f32[512,512]{1,0:T(8,128)} %collective-permute-done.5.refs_0_, f32[512,512]{1,0:T(8,128)S(1)} %collective-permute-done.refs_1_, f32[512,512]{1,0:T(8,128)} %collective-permute-done.4.refs_2_), custom_call_target="tpu_custom_call" | custom-call | flops 805306368 | bytes 4194304 | tf_op jit(solution)/shard_map/pallas_call | solution.py:334
  127.7 3.2 %shard_map.85 = f32[2,8,2,32,256]{4,3,2,1,0:T(8,128)S(1)} custom-call(s32[8]{0:T(128)S(1)} %stack.30.me_ref, f32[512,512]{1,0:T(8,128)} %collective-permute-done.5.refs_0_, f32[512,512]{1,0:T(8,128)S(1)} %collective-permute-done.refs_1_, f32[512,512]{1,0:T(8,128)} %collective-permute-done.4.refs_2_), custom_call_target="tpu_custom_call" | custom-call | flops 805306368 | bytes 4194304 | tf_op jit(solution)/shard_map/pallas_call | solution.py:334
  132.1 7.4 %all-to-all-start.4 = ((f32[16,2,32,256]{3,2,1,0:T(8,128)}), f32[16,2,32,256]{3,2,1,0:T(8,128)S(1)}, u32[]{:S(2)}, u32[]{:S(2)}) async-start(f32[16,2,32,256]{3,2,1,0:T(8,128)} %bitcast.24), calls=%async_computation.4 | async-start | bytes 2097152 | tf_op jit(solution)/shard_map/all_to_all | solution.py:347
  140.9 2.6 %collective-permute-start.8 = (f32[1,32,256]{2,1,0:T(8,128)S(1)}, f32[1,32,256]{2,1,0:T(8,128)S(1)}, u32[]{:S(2)}, u32[]{:S(2)}) collective-permute-start(f32[1,32,256]{2,1,0:T(8,128)S(1)} %slice.8), channel_id=1, source_target_pairs={{0,224},{32,0},{64,32},{96,64},{128,96},{160,128},{192,160},{224,1... | collective-permute-start | bytes 98312 | tf_op jit(solution)/shard_map/ppermute | solution.py:278
  145.1 3.3 %collective-permute-done.7.up1 = f32[2,32,256]{2,1,0:T(8,128)S(1)} collective-permute-done((f32[2,32,256]{2,1,0:T(8,128)S(1)}, f32[2,32,256]{2,1,0:T(8,128)S(1)}, u32[]{:S(2)}, u32[]{:S(2)}) %collective-permute-start.7) | collective-permute-done | bytes 65568 | tf_op jit(solution)/shard_map/ppermute | solution.py:286
  148.3 7.5 %all-to-all-done.4.parts_ref = f32[16,2,32,256]{3,2,1,0:T(8,128)S(1)} async-done(((f32[16,2,32,256]{3,2,1,0:T(8,128)}), f32[16,2,32,256]{3,2,1,0:T(8,128)S(1)}, u32[]{:S(2)}, u32[]{:S(2)}) %all-to-all-start.4) | async-done | bytes 1048608 | tf_op jit(solution)/shard_map/all_to_all | solution.py:347
  155.8 3.0 %collective-permute-start.11 = (f32[256,512]{1,0:T(8,128)S(1)}, f32[256,512]{1,0:T(8,128)S(1)}, u32[]{:S(2)}, u32[]{:S(2)}) collective-permute-start(f32[256,512]{1,0:T(8,128)S(1)} %copy-done.1), channel_id=1, source_target_pairs={{0,16},{16,0},{1,17},{17,1},{2,18},{18,2},{3,19},{19,3},{4,20},{20... | collective-permute-start | bytes 1572872 | tf_op jit(solution)/shard_map/ppermute | solution.py:274
  161.1 5.1 %collective-permute-done.10.far_up1 = f32[1,32,256]{2,1,0:T(8,128)S(1)} collective-permute-done((f32[1,32,256]{2,1,0:T(8,128)S(1)}, f32[1,32,256]{2,1,0:T(8,128)S(1)}, u32[]{:S(2)}, u32[]{:S(2)}) %collective-permute-start.10) | collective-permute-done | bytes 32800 | tf_op jit(solution)/shard_map/ppermute | solution.py:286
  167.5 3.7 %all-to-all-start.5 = ((f32[8,32,256]{2,1,0:T(8,128)}), f32[8,32,256]{2,1,0:T(8,128)S(1)}, u32[]{:S(2)}, u32[]{:S(2)}) async-start(f32[8,32,256]{2,1,0:T(8,128)} %shard_map.88), calls=%async_computation.5 | async-start | bytes 524288 | tf_op jit(solution)/shard_map/all_to_all | solution.py:367
  173.0 5.5 %all-to-all-done.5 = f32[8,32,256]{2,1,0:T(8,128)S(1)} async-done(((f32[8,32,256]{2,1,0:T(8,128)}), f32[8,32,256]{2,1,0:T(8,128)S(1)}, u32[]{:S(2)}, u32[]{:S(2)}) %all-to-all-start.5) | async-done | bytes 262176 | tf_op jit(solution)/shard_map/all_to_all | solution.py:367
  (36 shorter events, 20.7 us)
Async XLA Ops:
  3.4 33.8 %copy-start = (s32[256]{0:T(256)S(1)}, s32[256]{0:T(256)}, u32[]{:S(2)}) copy-start(s32[256]{0:T(256)} %cell_ref.1) | copy-start | bytes 3076
  3.4 33.8 %all-to-all-start = ((f32[16,33,8,128]{3,2,1,0:T(8,128)}), f32[16,33,8,128]{3,2,1,0:T(8,128)S(1)}, u32[]{:S(2)}, u32[]{:S(2)}) async-start(f32[16,33,8,128]{3,2,1,0:T(8,128)} %shard_map.77), calls=%async_computation | async-start | bytes 4325376 | tf_op jit(solution)/shard_map/all_to_all | solution.py:314
  63.3 28.5 %collective-permute-start = (f32[512,512]{1,0:T(8,128)S(1)}, f32[512,512]{1,0:T(8,128)S(1)}, u32[]{:S(2)}, u32[]{:S(2)}) collective-permute-start(f32[512,512]{1,0:T(8,128)S(1)} %bitcast.15), channel_id=1, source_target_pairs={{0,224},{32,0},{64,32},{96,64},{128,96},{160,128},{192,160},{224,1... | collective-permute-start | bytes 3145736 | tf_op jit(solution)/shard_map/ppermute | solution.py:278
  69.2 26.0 %collective-permute-start.1 = (f32[512,512]{1,0:T(8,128)S(1)}, f32[512,512]{1,0:T(8,128)S(1)}, u32[]{:S(2)}, u32[]{:S(2)}) collective-permute-start(f32[512,512]{1,0:T(8,128)S(1)} %bitcast.16), channel_id=1, source_target_pairs={{0,32},{32,64},{64,96},{96,128},{128,160},{160,192},{192,224},{224... | collective-permute-start | bytes 3145736 | tf_op jit(solution)/shard_map/ppermute | solution.py:278
  70.6 2.0 %collective-permute-start.2 = (f32[2,8,1,32,256]{4,3,2,1,0:T(8,128)S(1)}, f32[2,8,1,32,256]{4,3,2,1,0:T(8,128)S(1)}, u32[]{:S(2)}, u32[]{:S(2)}) collective-permute-start(f32[2,8,1,32,256]{4,3,2,1,0:T(8,128)S(1)} %shard_map.80), channel_id=1, source_target_pairs={{0,1},{1,0},{2,3},{3,2},{4,5},{5,4},{6,7},{7,6},{8,9},{9,8},{10,11... | collective-permute-start | bytes 1572872 | tf_op jit(solution)/shard_map/ppermute | solution.py:274
  73.4 16.2 %all-to-all-start.2 = ((f32[16,1,32,256]{3,2,1,0:T(8,128)}), f32[16,1,32,256]{3,2,1,0:T(8,128)}, u32[]{:S(2)}, u32[]{:S(2)}) async-start(f32[16,1,32,256]{3,2,1,0:T(8,128)} %bitcast.26), calls=%async_computation.2 | async-start | bytes 1048576 | tf_op jit(solution)/shard_map/all_to_all | solution.py:347
  97.3 4.3 %collective-permute-start.3 = (f32[2,8,2,32,256]{4,3,2,1,0:T(8,128)S(1)}, f32[2,8,2,32,256]{4,3,2,1,0:T(8,128)S(1)}, u32[]{:S(2)}, u32[]{:S(2)}) collective-permute-start(f32[2,8,2,32,256]{4,3,2,1,0:T(8,128)S(1)} %shard_map.83), channel_id=1, source_target_pairs={{0,1},{1,0},{2,3},{3,2},{4,5},{5,4},{6,7},{7,6},{8,9},{9,8},{10,11... | collective-permute-start | bytes 3145736 | tf_op jit(solution)/shard_map/ppermute | solution.py:274
  97.4 25.7 %collective-permute-start.4 = (f32[512,512]{1,0:T(8,128)S(1)}, f32[512,512]{1,0:T(8,128)}, u32[]{:S(2)}, u32[]{:S(2)}) collective-permute-start(f32[512,512]{1,0:T(8,128)S(1)} %collective-permute-done.refs_1_), channel_id=1, source_target_pairs={{0,224},{32,0},{64,32},{96,64},{128,96},{160,128},{192,160},{224,1... | collective-permute-start | bytes 3145736 | tf_op jit(solution)/shard_map/ppermute | solution.py:278
  97.8 26.5 %collective-permute-start.5 = (f32[512,512]{1,0:T(8,128)S(1)}, f32[512,512]{1,0:T(8,128)}, u32[]{:S(2)}, u32[]{:S(2)}) collective-permute-start(f32[512,512]{1,0:T(8,128)S(1)} %collective-permute-done.1.refs_2_), channel_id=1, source_target_pairs={{0,32},{32,64},{64,96},{96,128},{128,160},{160,192},{192,224},{224... | collective-permute-start | bytes 3145736 | tf_op jit(solution)/shard_map/ppermute | solution.py:278
  102.8 21.6 %all-to-all-start.3 = ((f32[16,2,32,256]{3,2,1,0:T(8,128)}), f32[16,2,32,256]{3,2,1,0:T(8,128)}, u32[]{:S(2)}, u32[]{:S(2)}) async-start(f32[16,2,32,256]{3,2,1,0:T(8,128)} %bitcast.25), calls=%async_computation.3 | async-start | bytes 2097152 | tf_op jit(solution)/shard_map/all_to_all | solution.py:347
  127.6 3.3 %collective-permute-start.6 = (f32[2,8,2,32,256]{4,3,2,1,0:T(8,128)S(1)}, f32[2,8,2,32,256]{4,3,2,1,0:T(8,128)S(1)}, u32[]{:S(2)}, u32[]{:S(2)}) collective-permute-start(f32[2,8,2,32,256]{4,3,2,1,0:T(8,128)S(1)} %shard_map.86), channel_id=1, source_target_pairs={{0,1},{1,0},{2,3},{3,2},{4,5},{5,4},{6,7},{7,6},{8,9},{9,8},{10,11... | collective-permute-start | bytes 3145736 | tf_op jit(solution)/shard_map/ppermute | solution.py:274
  132.1 23.7 %copy-start.1 = (f32[256,512]{1,0:T(8,128)S(1)}, f32[256,512]{1,0:T(8,128)}, u32[]{:S(2)}) copy-start(f32[256,512]{1,0:T(8,128)} %constant_dynamic-slice_fusion) | copy-start | bytes 1572868
  132.1 23.7 %all-to-all-start.4 = ((f32[16,2,32,256]{3,2,1,0:T(8,128)}), f32[16,2,32,256]{3,2,1,0:T(8,128)S(1)}, u32[]{:S(2)}, u32[]{:S(2)}) async-start(f32[16,2,32,256]{3,2,1,0:T(8,128)} %bitcast.24), calls=%async_computation.4 | async-start | bytes 2097152 | tf_op jit(solution)/shard_map/all_to_all | solution.py:347
  140.8 7.5 %collective-permute-start.7 = (f32[2,32,256]{2,1,0:T(8,128)S(1)}, f32[2,32,256]{2,1,0:T(8,128)S(1)}, u32[]{:S(2)}, u32[]{:S(2)}) collective-permute-start(f32[2,32,256]{2,1,0:T(8,128)S(1)} %shard_map.84.d12), channel_id=1, source_target_pairs={{0,32},{1,48},{16,33},{17,49},{32,64},{33,80},{48,65},{49,81},{64,... | collective-permute-start | bytes 196616 | tf_op jit(solution)/shard_map/ppermute | solution.py:286
  140.9 4.2 %collective-permute-start.8 = (f32[1,32,256]{2,1,0:T(8,128)S(1)}, f32[1,32,256]{2,1,0:T(8,128)S(1)}, u32[]{:S(2)}, u32[]{:S(2)}) collective-permute-start(f32[1,32,256]{2,1,0:T(8,128)S(1)} %slice.8), channel_id=1, source_target_pairs={{0,224},{32,0},{64,32},{96,64},{128,96},{160,128},{192,160},{224,1... | collective-permute-start | bytes 98312 | tf_op jit(solution)/shard_map/ppermute | solution.py:278
  155.8 15.4 %collective-permute-start.11 = (f32[256,512]{1,0:T(8,128)S(1)}, f32[256,512]{1,0:T(8,128)S(1)}, u32[]{:S(2)}, u32[]{:S(2)}) collective-permute-start(f32[256,512]{1,0:T(8,128)S(1)} %copy-done.1), channel_id=1, source_target_pairs={{0,16},{16,0},{1,17},{17,1},{2,18},{18,2},{3,19},{19,3},{4,20},{20... | collective-permute-start | bytes 1572872 | tf_op jit(solution)/shard_map/ppermute | solution.py:274
  158.9 7.4 %collective-permute-start.9 = (f32[2,32,256]{2,1,0:T(8,128)S(1)}, f32[2,32,256]{2,1,0:T(8,128)S(1)}, u32[]{:S(2)}, u32[]{:S(2)}) collective-permute-start(f32[2,32,256]{2,1,0:T(8,128)S(1)} %shard_map.87), channel_id=1, source_target_pairs={{0,192},{32,224},{64,0},{96,32},{128,64},{160,96},{192,128},{224,1... | collective-permute-start | bytes 196616 | tf_op jit(solution)/shard_map/ppermute | solution.py:278
  159.2 7.1 %collective-permute-start.10 = (f32[1,32,256]{2,1,0:T(8,128)S(1)}, f32[1,32,256]{2,1,0:T(8,128)S(1)}, u32[]{:S(2)}, u32[]{:S(2)}) collective-permute-start(f32[1,32,256]{2,1,0:T(8,128)S(1)} %slice.9), channel_id=1, source_target_pairs={{0,32},{1,48},{16,33},{17,49},{32,64},{33,80},{48,65},{49,81},{64,... | collective-permute-start | bytes 98312 | tf_op jit(solution)/shard_map/ppermute | solution.py:286
  167.5 11.0 %all-to-all-start.5 = ((f32[8,32,256]{2,1,0:T(8,128)}), f32[8,32,256]{2,1,0:T(8,128)S(1)}, u32[]{:S(2)}, u32[]{:S(2)}) async-start(f32[8,32,256]{2,1,0:T(8,128)} %shard_map.88), calls=%async_computation.5 | async-start | bytes 524288 | tf_op jit(solution)/shard_map/all_to_all | solution.py:367
